TPU v7x, 128 devices: a whole 4x4x4 slice. The times are simulated.
128 devices in a mesh: blk: 8 (over y, core), sector: 16 (over x, z).
Axes of the slice: x: 4, y: 4, z: 4, core: 2. Of those that a mesh axis runs over, the one named last changes fastest.
Arguments:
- local_gap: float32 [8, 16, 64, 2048], P('blk', 'sector'), may hold values from -6 to 6
- previous: float32 [8, 16, 64, 2048], P('blk', 'sector'), may hold values from -6 to 6
- flexibility: bfloat16 [8, 16, 2048, 2048], P('blk', 'sector'), as said below
- schur: bfloat16 [8, 16, 2048, 2048], P('blk', 'sector'), as said below
- corner_flex: bfloat16 [8, 16, 24, 2048], P('blk', 'sector'), may hold values from -0.375 to 0.375
- coarse_inverse: float32 [864, 864], P('sector'), as said below
- scaling: float32 [8, 16, 2048], P('blk', 'sector'), may hold values from 0.2 to 2
- counts: int32 [8, 16, 4], P('blk', 'sector'), may hold values from 0 to 512, as said below
- matching: int32 [8, 16, 2048], P('blk', 'sector'), may hold values from 0 to 511, as said below
- corner_map: int32 [8, 16, 24], P('blk', 'sector'), may hold values from 0 to 863, as said below
Outputs:
- multipliers: float32 [8, 16, 64, 2048], P('blk', 'sector')
- residual: float32 [8, 16, 64, 2048], P('blk', 'sector')
- precond: float32 [8, 16, 64, 2048], P('blk', 'sector')
Inputs may be any that keep to these rules, and one draw needn't show every extreme that they name: `counts`: every face shared by two subdomains has between 128 and 512 slots in use, the same number on both sides; the lower face of the first cycle and the upper face of the last cycle have none; some face has exactly 512. On every face the slots in use are matched one to one with the slots in use of the neighbour's opposite face, and the neighbour's matching is the inverse of this one; slots not in use hold some index of the face. `corner_map`: component q of the corner node that subdomains share maps to the same coarse dof in each of them; the numbering of all corner nodes' components is one to one onto 0 to 863. `flexibility`: symmetric positive definite for every subdomain. `schur`: symmetric positive definite for every subdomain. `coarse_inverse`: symmetric positive definite.
All inputs are finite; a program needn't handle non-finite values.
Results may differ from a plain program's by a relative error of at most 0.0065.
The roundings to bfloat16 on the way count: a program that leaves them out, or rounds other values in their place, can miss the bound.
Values sent between devices are 32-bit elements; how exact they have to be, the bound alone decides.
No kernel may reach another device: no remote copies, remote signals or barrier semaphores. Data moves between devices by JAX's collectives and lax.ppermute only.
A program may use at most 128 MiB of HBM per device.

v0:
```python
import jax
import jax.numpy as jnp
from jax import lax
from jax.sharding import PartitionSpec as P

ITERS = 2


def shifted(block, axis, distance):
    devices = range(lax.axis_size(axis))
    route = [(i - distance, i) for i in devices if i - distance in devices]
    return lax.ppermute(block, axis, route)


def shifted_2(x, axis, by):
    count = lax.axis_size(axis)
    return lax.ppermute(x, axis, [(i, (i + by) % count) for i in range(count)])


def pick_rows(table, index):
    return jnp.take(table, index, axis=0)


def make_jump(match_faces, active):

    def jump(field):
        rows = field.shape[0]
        width = field.shape[1]
        face_size = width // 4
        faces = field.reshape(rows, 4, face_size)
        from_lower = shifted(faces[:, 1], "blk", 1)
        from_upper = shifted(faces[:, 0], "blk", -1)
        from_prev = shifted_2(faces[:, 3], "sector", 1)
        from_next = shifted_2(faces[:, 2], "sector", -1)
        beside = jnp.stack([from_lower, from_upper, from_prev, from_next], axis=0)
        slots_first = jnp.transpose(beside, (0, 2, 1))
        picked = jax.vmap(pick_rows)(slots_first, match_faces)
        picked = jnp.transpose(picked, (2, 0, 1)).reshape(rows, width)
        return (field - picked) * active[None, :]

    return jump


def body(
    local_gap,
    previous,
    flexibility,
    schur,
    corner_flex,
    coarse_inverse,
    scaling,
    counts,
    matching,
    corner_map,
):
    gap = local_gap[0, 0]
    prior = previous[0, 0]
    flex = flexibility[0, 0]
    dirichlet = schur[0, 0]
    corners = corner_flex[0, 0]
    weights = scaling[0, 0][None, :]
    width = gap.shape[1]
    face_size = width // 4
    active = (
        (jnp.arange(face_size)[None, :] < counts[0, 0][:, None]).astype(jnp.float32).reshape(width)
    )
    match_faces = matching[0, 0].reshape(4, face_size)
    jump = make_jump(match_faces, active)
    coarse_count = coarse_inverse.shape[1]
    onehot = (corner_map[0, 0][:, None] == jnp.arange(coarse_count)[None, :]).astype(jnp.float32)
    highest = lax.Precision.HIGHEST
    full_inverse = lax.all_gather(coarse_inverse, "sector", axis=0, tiled=True)

    def operator(field):
        rounded = field.astype(jnp.bfloat16)
        local = jnp.dot(rounded, flex, preferred_element_type=jnp.float32)
        corner_part = lax.dot_general(
            rounded, corners, (((1,), (1,)), ((), ())), preferred_element_type=jnp.float32
        )
        spread = jnp.dot(corner_part, onehot, precision=highest, preferred_element_type=jnp.float32)
        total = lax.psum(spread, ("blk", "sector"))
        coarse = jnp.dot(total, full_inverse, precision=highest, preferred_element_type=jnp.float32)
        back = lax.dot_general(
            coarse,
            onehot,
            (((1,), (1,)), ((), ())),
            precision=highest,
            preferred_element_type=jnp.float32,
        )
        back = back.astype(jnp.bfloat16)
        return local + jnp.dot(back, corners, preferred_element_type=jnp.float32)

    def preconditioned(residual, want_energy):
        scaled = (residual * weights).astype(jnp.bfloat16)
        weighted = jnp.dot(scaled, dirichlet, preferred_element_type=jnp.float32) * weights
        if not want_energy:
            return (jump(weighted), None)
        precond = jump(weighted)
        energy = lax.psum(jnp.sum(residual * precond, axis=1), ("blk", "sector"))
        return (precond, energy)

    start = 0.5 * jump(prior)
    residual = jump(gap - operator(start))
    precond, energy = preconditioned(residual, True)
    direction = precond
    multipliers = start
    for step in range(ITERS):
        response = operator(direction)
        image = jump(response)
        curvature = lax.psum(jnp.sum(direction * image, axis=1), ("blk", "sector"))
        alpha = (energy / curvature)[:, None]
        multipliers = multipliers + alpha * direction
        residual = residual - alpha * image
        last_step = step + 1 == ITERS
        precond, fresh = preconditioned(residual, not last_step)
        if not last_step:
            direction = precond + (fresh / energy)[:, None] * direction
            energy = fresh
    return (multipliers[None, None], residual[None, None], precond[None, None])


def solution(mesh):
    placed = (
        P("blk", "sector", None, None),
        P("blk", "sector", None, None),
        P("blk", "sector", None, None),
        P("blk", "sector", None, None),
        P("blk", "sector", None, None),
        P("sector", None),
        P("blk", "sector", None),
        P("blk", "sector", None),
        P("blk", "sector", None),
        P("blk", "sector", None),
    )
    return jax.shard_map(
        body,
        mesh=mesh,
        in_specs=placed,
        out_specs=(
            P("blk", "sector", None, None),
            P("blk", "sector", None, None),
            P("blk", "sector", None, None),
        ),
        check_vma=False,
    )
```

profile of v0, /device:TPU:1, one launch (start us, length us, event | category | flops | bytes accessed | tf_op | source)
XLA Modules:
  0.0 913.3 jit_solution(10326536690249211024)
XLA Ops:
  10.3 4.7 collective-permute-start
  15.0 6.0 collective-permute-start.3
  27.4 5.5 collective-permute-done.2
  34.6 13.0 %gather_fusion = f32[2048,64]{1,0:T(8,128)S(1)} fusion(f32[4,512,64]{2,1,0:T(8,128)S(1)} %maximum_bitcast_fusion, s32[2048]{0:T(1024)S(1)} %bitcast.226), kind=kCustom, calls=%fused_computation.clone | custom fusion | bytes 1064960 | tf_op jit(solution)/shard_map/vmap(jit(_take))/gather | solution.py:21
  50.0 5.8 fusion.10
  55.8 8.4 all-gather.3.cloned.1.call-done
  66.3 123.8 %all-reduce.5.cloned.1.call-done = f32[64,864]{1,0:T(8,128)} async-done(((f32[64,864]{1,0:T(8,128)}), f32[64,864]{1,0:T(8,128)}) %all-reduce.5.cloned.1.call-update) | async-done | bytes 221200 | tf_op jit(solution)/shard_map/psum | solution.py:81
  209.6 4.2 collective-permute-done.6
  213.9 13.0 %gather_fusion.1 = f32[2048,64]{1,0:T(8,128)S(1)} fusion(f32[4,512,64]{2,1,0:T(8,128)S(1)} %maximum_bitcast_fusion.1, s32[2048]{0:T(1024)S(1)} %bitcast.227), kind=kCustom, calls=%fused_computation.1.clone | custom fusion | bytes 1064960 | tf_op jit(solution)/shard_map/vmap(jit(_take))/gather | solution.py:21
  229.6 4.9 fusion.13
  235.0 4.3 collective-permute-start.8
  242.9 4.0 collective-permute-done.11
  250.4 13.0 %gather_fusion.2 = f32[2048,64]{1,0:T(8,128)S(1)} fusion(f32[4,512,64]{2,1,0:T(8,128)S(1)} %maximum_bitcast_fusion.2, s32[2048]{0:T(1024)S(1)} %bitcast.228), kind=kCustom, calls=%fused_computation.2.clone | custom fusion | bytes 1064960 | tf_op jit(solution)/shard_map/vmap(jit(_take))/gather | solution.py:21
  266.3 6.1 fusion.8
  272.3 130.4 %all-reduce.7.cloned.1.call-done = f32[64,864]{1,0:T(8,128)} async-done(((f32[64,864]{1,0:T(8,128)}), f32[64,864]{1,0:T(8,128)}) %all-reduce.7.cloned.1.call-update) | async-done | bytes 221200 | tf_op jit(solution)/shard_map/psum | solution.py:81
  418.3 4.2 collective-permute-done.14
  422.6 22.5 %gather_fusion.3 = f32[2048,64]{1,0:T(8,128)} fusion(f32[4,512,64]{2,1,0:T(8,128)S(1)} %maximum_bitcast_fusion.3, s32[2048]{0:T(1024)S(1)} %bitcast.229), kind=kCustom, calls=%fused_computation.3.clone | custom fusion | bytes 1064960 | tf_op jit(solution)/shard_map/vmap(jit(_take))/gather | solution.py:21
  447.3 63.4 %all-reduce = (f32[64]{0:T(128)S(1)}, f32[64]{0:T(128)S(1)}) all-reduce(f32[64]{0:T(128)S(1)} %get-tuple-element.5, f32[64]{0:T(128)S(1)} %get-tuple-element.4), channel_id=1, replica_groups=mesh['blk'=8,'sector'=16] {'blk','sector'}, use_global_device_ids=true, to_apply=%region_2.4 | all-reduce | flops 128 | bytes 1024 | tf_op jit(solution)/shard_map/psum | solution.py:99
  510.9 5.2 fusion.16
  523.7 3.7 collective-permute-done.19
  527.5 3.9 collective-permute-done.18
  531.4 22.5 %gather_fusion.4 = f32[2048,64]{1,0:T(8,128)} fusion(f32[4,512,64]{2,1,0:T(8,128)S(1)} %maximum_bitcast_fusion.4, s32[2048]{0:T(1024)S(1)} %bitcast.230), kind=kCustom, calls=%fused_computation.4.clone | custom fusion | bytes 1064960 | tf_op jit(solution)/shard_map/vmap(jit(_take))/gather | solution.py:21
  556.0 63.3 %psum.53 = f32[64]{0:T(128)S(1)} all-reduce(f32[64]{0:T(128)S(1)} %multiply_reduce_fusion.1), channel_id=1, replica_groups=mesh['blk'=8,'sector'=16] {'blk','sector'}, use_global_device_ids=true, to_apply=%region_7.9 | all-reduce | flops 64 | bytes 512 | tf_op jit(solution)/shard_map/psum | solution.py:99
  621.5 6.1 fusion.6
  627.6 131.5 %all-reduce.9.cloned.1.call-done = f32[64,864]{1,0:T(8,128)} async-done(((f32[64,864]{1,0:T(8,128)}), f32[64,864]{1,0:T(8,128)}) %all-reduce.9.cloned.1.call-update) | async-done | bytes 221200 | tf_op jit(solution)/shard_map/psum | solution.py:81
  774.6 4.2 collective-permute-done.22
  778.9 22.6 %gather_fusion.5 = f32[2048,64]{1,0:T(8,128)} fusion(f32[4,512,64]{2,1,0:T(8,128)S(1)} %maximum_bitcast_fusion.5, s32[2048]{0:T(1024)S(1)} %bitcast.231), kind=kCustom, calls=%fused_computation.5.clone | custom fusion | bytes 1064960 | tf_op jit(solution)/shard_map/vmap(jit(_take))/gather | solution.py:21
  803.6 63.6 %psum.55 = f32[64]{0:T(128)S(1)} all-reduce(f32[64]{0:T(128)S(1)} %multiply_reduce_fusion), channel_id=1, replica_groups=mesh['blk'=8,'sector'=16] {'blk','sector'}, use_global_device_ids=true, to_apply=%region_10.12 | all-reduce | flops 64 | bytes 512 | tf_op jit(solution)/shard_map/psum | solution.py:110
  870.4 4.9 fusion.19
  882.8 3.9 collective-permute-done.27
  886.8 3.9 collective-permute-done.26
  890.7 13.0 %gather_fusion.6 = f32[2048,64]{1,0:T(8,128)S(1)} fusion(f32[4,512,64]{2,1,0:T(8,128)S(1)} %maximum_bitcast_fusion.6, s32[2048]{0:T(1024)S(1)} %bitcast.232), kind=kCustom, calls=%fused_computation.6.clone | custom fusion | bytes 1064960 | tf_op jit(solution)/shard_map/vmap(jit(_take))/gather | solution.py:21
  (171 shorter events, 106.7 us)
Async XLA Ops:
  8.0 56.2 %all-gather.3.cloned.1.call-start = ((), (), s32[]{:S(2)}) async-start(), calls=%async_computation.3 | async-start | bytes 3411968 | tf_op jit(solution)/shard_map/all_gather | solution.py:72
  8.7 181.3 %all-reduce.5.cloned.1.call-start = ((), (), s32[]{:S(2)}) async-start(), calls=%async_computation | async-start | bytes 458752 | tf_op jit(solution)/shard_map/psum | solution.py:81
  10.3 15.4 %collective-permute-start = (f32[64,512]{0,1:T(8,128)S(1)}, f32[64,512]{0,1:T(8,128)S(1)}, u32[]{:S(2)}, u32[]{:S(2)}) collective-permute-start(f32[64,512]{0,1:T(8,128)S(1)} %get-tuple-element.32), channel_id=1, source_target_pairs={{0,16},{16,32},{32,48},{48,64},{64,80},{80,96},{96,112},{1,17},{17... | collective-permute-start | bytes 393224 | tf_op jit(solution)/shard_map/ppermute | solution.py:12
  15.0 12.4 %collective-permute-start.3 = (f32[64,512]{0,1:T(8,128)S(1)}, f32[64,512]{0,1:T(8,128)S(1)}, u32[]{:S(2)}, u32[]{:S(2)}) collective-permute-start(f32[64,512]{0,1:T(8,128)S(1)} %get-tuple-element.33), channel_id=1, source_target_pairs={{0,15},{1,0},{2,1},{3,2},{4,3},{5,4},{6,5},{7,6},{8,7},{9,8},{10,9... | collective-permute-start | bytes 393224 | tf_op jit(solution)/shard_map/ppermute | solution.py:17
  21.0 11.8 %collective-permute-start.2 = (f32[64,512]{0,1:T(8,128)S(1)}, f32[64,512]{0,1:T(8,128)S(1)}, u32[]{:S(2)}, u32[]{:S(2)}) collective-permute-start(f32[64,512]{0,1:T(8,128)S(1)} %get-tuple-element.34), channel_id=1, source_target_pairs={{0,1},{1,2},{2,3},{3,4},{4,5},{5,6},{6,7},{7,8},{8,9},{9,10},{10,1... | collective-permute-start | bytes 393224 | tf_op jit(solution)/shard_map/ppermute | solution.py:17
  21.0 11.8 %collective-permute-start.1 = (f32[64,512]{0,1:T(8,128)S(1)}, f32[64,512]{0,1:T(8,128)S(1)}, u32[]{:S(2)}, u32[]{:S(2)}) collective-permute-start(f32[64,512]{0,1:T(8,128)S(1)} %get-tuple-element.35), channel_id=1, source_target_pairs={{16,0},{32,16},{48,32},{64,48},{80,64},{96,80},{112,96},{17,1},{33... | collective-permute-start | bytes 393224 | tf_op jit(solution)/shard_map/ppermute | solution.py:12
  49.9 352.9 %all-reduce.7.cloned.1.call-start = ((), (), s32[]{:S(2)}) async-start(), calls=%async_computation.1 | async-start | bytes 458752 | tf_op jit(solution)/shard_map/psum | solution.py:81
  199.0 7.2 collective-permute-start.4
  201.5 8.1 collective-permute-start.7
  203.5 10.4 %collective-permute-start.6 = (f32[64,512]{0,1:T(8,128)S(1)}, f32[64,512]{0,1:T(8,128)S(1)}, u32[]{:S(2)}, u32[]{:S(2)}) collective-permute-start(f32[64,512]{0,1:T(8,128)S(1)} %get-tuple-element.30), channel_id=1, source_target_pairs={{0,1},{1,2},{2,3},{3,4},{4,5},{5,6},{6,7},{7,8},{8,9},{9,10},{10,1... | collective-permute-start | bytes 393224 | tf_op jit(solution)/shard_map/ppermute | solution.py:17
  203.5 10.4 %collective-permute-start.5 = (f32[64,512]{0,1:T(8,128)S(1)}, f32[64,512]{0,1:T(8,128)S(1)}, u32[]{:S(2)}, u32[]{:S(2)}) collective-permute-start(f32[64,512]{0,1:T(8,128)S(1)} %get-tuple-element.31), channel_id=1, source_target_pairs={{16,0},{32,16},{48,32},{64,48},{80,64},{96,80},{112,96},{17,1},{33... | collective-permute-start | bytes 393224 | tf_op jit(solution)/shard_map/ppermute | solution.py:12
  235.0 7.9 collective-permute-start.8
  239.3 7.6 collective-permute-start.11
  239.3 11.0 %collective-permute-start.10 = (f32[64,512]{0,1:T(8,128)S(1)}, f32[64,512]{0,1:T(8,128)S(1)}, u32[]{:S(2)}, u32[]{:S(2)}) collective-permute-start(f32[64,512]{0,1:T(8,128)S(1)} %get-tuple-element.26), channel_id=1, source_target_pairs={{0,1},{1,2},{2,3},{3,4},{4,5},{5,6},{6,7},{7,8},{8,9},{9,10},{10,1... | collective-permute-start | bytes 393224 | tf_op jit(solution)/shard_map/ppermute | solution.py:17
  241.0 9.4 %collective-permute-start.9 = (f32[64,512]{0,1:T(8,128)S(1)}, f32[64,512]{0,1:T(8,128)S(1)}, u32[]{:S(2)}, u32[]{:S(2)}) collective-permute-start(f32[64,512]{0,1:T(8,128)S(1)} %get-tuple-element.27), channel_id=1, source_target_pairs={{16,0},{32,16},{48,32},{64,48},{80,64},{96,80},{112,96},{17,1},{33... | collective-permute-start | bytes 393224 | tf_op jit(solution)/shard_map/ppermute | solution.py:12
  266.2 492.9 %all-reduce.9.cloned.1.call-start = ((), (), s32[]{:S(2)}) async-start(), calls=%async_computation.2 | async-start | bytes 458752 | tf_op jit(solution)/shard_map/psum | solution.py:81
  407.6 7.3 collective-permute-start.12
  410.2 8.1 collective-permute-start.15
  412.2 10.4 %collective-permute-start.14 = (f32[64,512]{0,1:T(8,128)S(1)}, f32[64,512]{0,1:T(8,128)S(1)}, u32[]{:S(2)}, u32[]{:S(2)}) collective-permute-start(f32[64,512]{0,1:T(8,128)S(1)} %get-tuple-element.22), channel_id=1, source_target_pairs={{0,1},{1,2},{2,3},{3,4},{4,5},{5,6},{6,7},{7,8},{8,9},{9,10},{10,1... | collective-permute-start | bytes 393224 | tf_op jit(solution)/shard_map/ppermute | solution.py:17
  412.2 10.4 %collective-permute-start.13 = (f32[64,512]{0,1:T(8,128)S(1)}, f32[64,512]{0,1:T(8,128)S(1)}, u32[]{:S(2)}, u32[]{:S(2)}) collective-permute-start(f32[64,512]{0,1:T(8,128)S(1)} %get-tuple-element.23), channel_id=1, source_target_pairs={{16,0},{32,16},{48,32},{64,48},{80,64},{96,80},{112,96},{17,1},{33... | collective-permute-start | bytes 393224 | tf_op jit(solution)/shard_map/ppermute | solution.py:12
  516.5 7.3 collective-permute-start.16
  519.7 7.7 collective-permute-start.19
  520.9 10.4 %collective-permute-start.18 = (f32[64,512]{0,1:T(8,128)S(1)}, f32[64,512]{0,1:T(8,128)S(1)}, u32[]{:S(2)}, u32[]{:S(2)}) collective-permute-start(f32[64,512]{0,1:T(8,128)S(1)} %get-tuple-element.18), channel_id=1, source_target_pairs={{0,1},{1,2},{2,3},{3,4},{4,5},{5,6},{6,7},{7,8},{8,9},{9,10},{10,1... | collective-permute-start | bytes 393224 | tf_op jit(solution)/shard_map/ppermute | solution.py:17
  521.3 10.1 %collective-permute-start.17 = (f32[64,512]{0,1:T(8,128)S(1)}, f32[64,512]{0,1:T(8,128)S(1)}, u32[]{:S(2)}, u32[]{:S(2)}) collective-permute-start(f32[64,512]{0,1:T(8,128)S(1)} %get-tuple-element.19), channel_id=1, source_target_pairs={{16,0},{32,16},{48,32},{64,48},{80,64},{96,80},{112,96},{17,1},{33... | collective-permute-start | bytes 393224 | tf_op jit(solution)/shard_map/ppermute | solution.py:12
  763.9 9.3 %collective-permute-start.20 = (f32[64,512]{0,1:T(8,128)S(1)}, f32[64,512]{0,1:T(8,128)S(1)}, u32[]{:S(2)}, u32[]{:S(2)}) collective-permute-start(f32[64,512]{0,1:T(8,128)S(1)} %get-tuple-element.12), channel_id=1, source_target_pairs={{0,16},{16,32},{32,48},{48,64},{64,80},{80,96},{96,112},{1,17},{17... | collective-permute-start | bytes 393224 | tf_op jit(solution)/shard_map/ppermute | solution.py:12
  766.4 8.1 collective-permute-start.23
  768.4 10.4 %collective-permute-start.22 = (f32[64,512]{0,1:T(8,128)S(1)}, f32[64,512]{0,1:T(8,128)S(1)}, u32[]{:S(2)}, u32[]{:S(2)}) collective-permute-start(f32[64,512]{0,1:T(8,128)S(1)} %get-tuple-element.14), channel_id=1, source_target_pairs={{0,1},{1,2},{2,3},{3,4},{4,5},{5,6},{6,7},{7,8},{8,9},{9,10},{10,1... | collective-permute-start | bytes 393224 | tf_op jit(solution)/shard_map/ppermute | solution.py:17
  768.4 10.4 %collective-permute-start.21 = (f32[64,512]{0,1:T(8,128)S(1)}, f32[64,512]{0,1:T(8,128)S(1)}, u32[]{:S(2)}, u32[]{:S(2)}) collective-permute-start(f32[64,512]{0,1:T(8,128)S(1)} %get-tuple-element.15), channel_id=1, source_target_pairs={{16,0},{32,16},{48,32},{64,48},{80,64},{96,80},{112,96},{17,1},{33... | collective-permute-start | bytes 393224 | tf_op jit(solution)/shard_map/ppermute | solution.py:12
  875.8 7.1 collective-permute-start.24
  879.0 7.7 collective-permute-start.27
  880.2 10.4 %collective-permute-start.26 = (f32[64,512]{0,1:T(8,128)S(1)}, f32[64,512]{0,1:T(8,128)S(1)}, u32[]{:S(2)}, u32[]{:S(2)}) collective-permute-start(f32[64,512]{0,1:T(8,128)S(1)} %get-tuple-element.10), channel_id=1, source_target_pairs={{0,1},{1,2},{2,3},{3,4},{4,5},{5,6},{6,7},{7,8},{8,9},{9,10},{10,1... | collective-permute-start | bytes 393224 | tf_op jit(solution)/shard_map/ppermute | solution.py:17
  880.6 10.1 %collective-permute-start.25 = (f32[64,512]{0,1:T(8,128)S(1)}, f32[64,512]{0,1:T(8,128)S(1)}, u32[]{:S(2)}, u32[]{:S(2)}) collective-permute-start(f32[64,512]{0,1:T(8,128)S(1)} %get-tuple-element.11), channel_id=1, source_target_pairs={{16,0},{32,16},{48,32},{64,48},{80,64},{96,80},{112,96},{17,1},{33... | collective-permute-start | bytes 393224 | tf_op jit(solution)/shard_map/ppermute | solution.py:12
  (19 other events, 873.2 us)
Sparse Core Ops, SparseCore 0:
  11.0 53.0 all-gather.2
Sparse Core Ops, SparseCore 1:
  50.0 140.0 all-reduce.4
  266.3 136.4 all-reduce.6
  621.6 137.5 all-reduce.8
where the time goes:
time: 923 us; the launch traced here: 913 us
  waiting for transfers between devices  446 us (48%)
  blocking collectives  190 us (21%)
  local copies, waits for them, and re-layouts  142 us (15%)
  starting transfers between devices  56.7 us (6%)
  matrix products  50.6 us (5%)
  between operations  16.9 us (2%)
  other arithmetic  11 us (1%)
    psum x3, waiting for transfers between devices, operator(): total = lax.psum(spread, ('blk', 'sector'))  386 us
    psum x2, blocking collectives, preconditioned(): energy = lax.psum(jnp.sum(residual * precond, axis=1), ('blk', 'sector'))  127 us
    gather x14, local copies, waits for them, and re-layouts, pick_rows(): return jnp.take(table, index, axis=0)  126 us
    psum x1, blocking collectives, body(): curvature = lax.psum(jnp.sum(direction * image, axis=1), ('blk', 'sector'))  63.6 us
    ppermute x14, waiting for transfers between devices, shifted_2(): return lax.ppermute(x, axis, [(i, (i + by) % count) for i in range(count)])  51 us
    ppermute x14, starting transfers between devices, shifted(): return lax.ppermute(block, axis, route)  39.8 us
  transfers between devices with their start and end apart: 32, of which 18 were waited for; matrix products, arithmetic and copies ran while one was open for 5% of the time, Pallas kernels for 0%

commit v1 on v0

v1 whole, which is shorter than its diff:
```python
import functools

import jax
import jax.numpy as jnp
from jax import lax
from jax.experimental import pallas as pl
from jax.experimental.pallas import tpu as pltpu
from jax.sharding import PartitionSpec as P

BOTH = ("blk", "sector")
PAYLOAD = 16
LANES = 128
SPAN = 32
F32, BF16 = jnp.float32, jnp.bfloat16
VMEM_LIMIT = 12 * 1024 * 1024


def swap(block, axis, offset):
    count = lax.axis_size(axis)
    route = []
    for i in range(offset, count + offset, 2):
        one, two = i % count, (i + 1) % count
        route += [(one, two), (two, one)]
    return lax.ppermute(block, axis, route)


def core_groups(blk, sector):
    return [[b * sector + s for b in range(c, blk, 2) for s in range(sector)] for c in range(2)]


def parts_of(x, count):
    out = []
    for _ in range(count):
        head = x.astype(BF16)
        out.append(head)
        x = x - head.astype(F32)
    return out


def dot(a, b):
    return jnp.dot(a, b, preferred_element_type=F32)


def dot_nt(a, b):
    return lax.dot_general(a, b, (((1,), (1,)), ((), ())), preferred_element_type=F32)


def dot_tn(a, b):
    return lax.dot_general(a, b, (((0,), (0,)), ((), ())), preferred_element_type=F32)


def columns(order, link, face):
    return pl.ds(pl.multiple_of(order[link] * face, face), face)


def picked(came, picker, link, rows):
    stacked = jnp.concatenate(parts_of(came[link][0:rows, :], 3), axis=0)
    got = dot(stacked, picker[link])
    return got[:rows] + got[rows : 2 * rows] + got[2 * rows :]


def column(row, rows):
    return jnp.transpose(jnp.broadcast_to(row, (LANES, LANES)))[:rows]


def take_rows(taken, which, row):
    number = column(row, SPAN)
    lane = lax.broadcasted_iota(jnp.int32, (SPAN, LANES), 1).astype(F32)
    for at in range(0, taken.shape[1], LANES):
        hit = jnp.where(number == lane + float(at), 1.0, 0.0)
        taken[which * SPAN : (which + 1) * SPAN, at : at + LANES] = hit.astype(BF16)


def flex_kernel(mode, order, *refs):
    refs = list(refs)
    came = [refs.pop(0) for _ in range(4)]
    field, picker, active, flex, corners = [refs.pop(0) for _ in range(5)]
    if mode == 0:
        gap, extra, numbers = refs.pop(0), refs.pop(0), refs.pop(0)
    if mode >= 1:
        energy = refs.pop(0)
    if mode == 2:
        old = refs.pop(0)
    p_out, h_out = refs.pop(0), refs.pop(0)
    links = [refs.pop(0) for _ in range(4)]
    if mode == 0:
        corner_faces, taken = refs.pop(1), refs.pop(1)
    payload, stack = refs
    rows, width = field.shape
    face = width // 4
    for link in range(4):
        cols = columns(order, link, face)
        p = field[:, cols] * active[:, cols] - picked(came, picker, link, rows)
        if mode == 0:
            p = 0.5 * p
        p_out[:, cols] = p
        if mode == 2:
            head, rest = parts_of(p, 2)
            stack[0:rows, cols] = head
            stack[rows : 2 * rows, cols] = rest
        else:
            stack[:, cols] = p.astype(BF16)
    if mode == 0:
        take_rows(taken, 0, numbers[0:1, 0:LANES])
        for link in range(4):
            cols = columns(order, link, face)
            own = corners[:, cols].astype(F32) * active[:, cols]
            theirs = dot(came[link][rows : rows + SPAN, :].astype(BF16), picker[link])
            corner_faces[link, 0:SPAN, :] = own.astype(BF16)
            corner_faces[link, SPAN : 2 * SPAN, :] = (-theirs).astype(BF16)
            take_rows(taken, link + 1, came[link][rows + SPAN : rows + SPAN + 1, 0:LANES])
    part = dot_nt(corners[...], stack[...])
    inner = jnp.zeros((rows, 1), F32)
    cross = jnp.zeros((rows, 1), F32)
    for link in range(4):
        cols = columns(order, link, face)
        local = dot(stack[...], flex[:, cols])
        if mode == 2:
            local = local[:rows] + local[rows:]
        p = p_out[:, cols]
        if mode == 0:
            local = gap[:, cols] - local
        else:
            inner = inner + jnp.sum(p * local, axis=1, keepdims=True)
        if mode == 2:
            cross = cross + jnp.sum(p * old[:, cols], axis=1, keepdims=True)
        h_out[:, cols] = local
        links[link][...] = local
    if mode == 2:
        part = part[:, :rows] + part[:, rows:]
    payload[0:16, 0:rows] = part[0:16]
    payload[0:8, rows : 2 * rows] = part[16:24]
    if mode == 0:
        scalars = extra[...]
    else:
        lane = lax.broadcasted_iota(jnp.int32, (rows, LANES), 1)
        table = jnp.where(lane == 0, energy[...], jnp.where(lane == 1, inner, 0.0))
        table = jnp.where(lane == 2, cross, table)
        scalars = jnp.transpose(table)[0:8]
    payload[8:16, rows : 2 * rows] = scalars


def first_kernel(order, prior, corners, numbers, *links):
    rows, width = prior.shape
    face = width // 4
    for link in range(4):
        cols = columns(order, link, face)
        links[link][0:rows, :] = prior[:, cols]
        links[link][rows : rows + SPAN, :] = corners[:, cols].astype(F32)
        links[link][rows + SPAN :, :] = numbers[...]


def picker_kernel(order, matching, active, flex, dirichlet, picker):
    face = picker.shape[1]
    source = lax.broadcasted_iota(jnp.int32, (face, face), 0)
    for link in range(4):
        cols = columns(order, link, face)
        hit = (source == matching[:, cols]) & (active[:, cols] > 0.5)
        picker[link] = jnp.where(hit, 1.0, 0.0).astype(BF16)


def assemble_kernel(mode, *refs):
    if mode == 0:
        got, places, out, spots = refs[0], refs[1], refs[-2], refs[-1]
        count = spots.shape[1]
        source = lax.broadcasted_iota(jnp.int32, (LANES, got.shape[0]), 0)
        for which in range(2):
            for at in range(0, count, LANES):
                hit = source + at == places[which : which + 1, :]
                spots[which, at : at + LANES, :] = jnp.where(hit, 1.0, 0.0).astype(BF16)
    else:
        got, spots, out = refs[0], refs[1], refs[-1]
    members = got.shape[0] // PAYLOAD
    half = spots.shape[1] // 2
    both = jnp.concatenate(parts_of(got[...], 2), axis=1)
    low = dot(spots[0], both)
    high = dot(spots[1], both)
    low = low[:, :LANES] + low[:, LANES:]
    high = high[:, :LANES] + high[:, LANES:]
    spread = low + pltpu.roll(high, LANES // 2, 1)
    lane = lax.broadcasted_iota(jnp.int32, (half, LANES), 1)
    out[0:half, :] = jnp.where(
        lane < LANES // 2, spread[:half], pltpu.roll(spread[half:], LANES // 2, 1)
    )
    total = jnp.sum(got[...].reshape(members, PAYLOAD, LANES), axis=0)
    out[half : half + 8, :] = total[8:16]


def coarse_kernel(mode, *refs):
    refs = list(refs)
    mine, theirs, taken = refs.pop(0), refs.pop(0), refs.pop(0)
    if mode == 0:
        inverse, back_out, head, rest = refs
        for at in range(0, inverse.shape[0], LANES):
            one, two = parts_of(inverse[at : at + LANES, :], 2)
            head[at : at + LANES, :] = one
            rest[at : at + LANES, :] = two
    else:
        head, rest = refs.pop(0), refs.pop(0)
    if mode == 1:
        back_out, alpha_out, spread_out, sums_out = refs
    if mode == 2:
        spread_old, sums_old, back_out, alpha_out, beta_out = refs
    rows = LANES // 2
    count = taken.shape[1]
    half = count // 2
    shift = LANES // 2
    total = mine[...] + theirs[...]
    spread = jnp.concatenate([total[:half], pltpu.roll(total[:half], shift, 1)], axis=0)
    sums = pltpu.roll(total[half:], shift, 1)
    valid = lax.broadcasted_iota(jnp.int32, (count, LANES), 1) < shift
    valid_row = lax.broadcasted_iota(jnp.int32, (1, LANES), 1) < shift
    spread = jnp.where(valid, spread, 0.0)
    if mode >= 1:
        energy, inner = sums[0:1], sums[1:2]
    if mode == 1:
        spread_out[...] = spread
        sums_out[...] = sums
    if mode == 2:
        beta = jnp.where(valid_row, energy / sums_old[0:1, :], 0.0)
        spread = spread + beta * spread_old[...]
        inner = inner + beta * (2.0 * sums[2:3] + beta * sums_old[1:2, :])
        beta_out[...] = column(beta, rows)
    first = spread.astype(BF16)
    second = spread - first.astype(F32)
    pair = (first.astype(F32) + pltpu.roll(second, shift, 1)).astype(BF16)
    coarse = dot(head[...], pair)
    coarse = coarse + pltpu.roll(coarse, shift, 1) + dot(rest[...], first)
    coarse = jnp.where(valid, coarse, 0.0)
    if mode >= 1:
        quad = jnp.sum(spread * coarse, axis=0, keepdims=True)
        alpha_out[...] = column(jnp.where(valid_row, energy / (inner + quad), 0.0), rows)
    one, two, three = parts_of(coarse, 3)
    pair = (one.astype(F32) + pltpu.roll(two.astype(F32), shift, 1)).astype(BF16)
    back = dot(taken[...], jnp.concatenate([pair, three], axis=1))
    low = back[:, :LANES]
    back_out[...] = low + pltpu.roll(low, shift, 1) + back[:, LANES:]


def schur_kernel(mode, order, *refs):
    refs = list(refs)
    back = refs.pop(0)
    came = [refs.pop(0) for _ in range(4)]
    field, picker, active, corner_faces, dirichlet, weights = [refs.pop(0) for _ in range(6)]
    if mode >= 1:
        alpha, before, direction, multipliers = [refs.pop(0) for _ in range(4)]
        alpha = alpha[:, 0:1]
    if mode == 2:
        beta, image_old, old = [refs.pop(0) for _ in range(3)]
        beta = beta[:, 0:1]
    residual, weighted = refs.pop(0), refs.pop(0)
    links = [refs.pop(0) for _ in range(4)]
    if mode <= 1:
        energy_out = refs.pop(0)
    if mode >= 1:
        mult_out = refs.pop(0)
    if mode == 1:
        image_out = refs.pop(0)
    (scaled,) = refs
    rows, width = field.shape
    face = width // 4
    back = back[...][:, :rows].astype(BF16)

    for link in range(4):
        cols = columns(order, link, face)
        jumped = field[:, cols] * active[:, cols] - picked(came, picker, link, rows)
        pieces = [back[0:SPAN], back[(link + 1) * SPAN : (link + 2) * SPAN]]
        behind = dot_tn(jnp.concatenate(pieces, axis=0), corner_faces[link])
        if mode == 0:
            now = jumped - behind
        else:
            d = direction[:, cols]
            if mode == 1:
                image_out[:, cols] = jumped
            else:
                jumped = jumped + beta * image_old[:, cols]
                d = d + beta * old[:, cols]
            mult_out[:, cols] = multipliers[:, cols] + alpha * d
            now = before[:, cols] - alpha * (jumped + behind)
        residual[:, cols] = now
        scaled[:, cols] = (now * weights[:, cols]).astype(BF16)
    energy = jnp.zeros((rows, 1), F32)
    for link in range(4):
        cols = columns(order, link, face)
        w = dot(scaled[...], dirichlet[:, cols]) * weights[:, cols]
        weighted[:, cols] = w
        links[link][...] = w
        if mode <= 1:
            energy = energy + jnp.sum(residual[:, cols] * w, axis=1, keepdims=True)
    if mode <= 1:
        energy_out[...] = jnp.broadcast_to(energy, (rows, LANES))


def last_kernel(order, *refs):
    came, (field, picker, active, out) = refs[:4], refs[4:]
    rows, width = field.shape
    for link in range(4):
        cols = columns(order, link, width // 4)
        out[:, cols] = field[:, cols] * active[:, cols] - picked(came, picker, link, rows)


def call(kernel, order, arrays, shapes, scratch=(), flops=0):
    where = pl.BlockSpec(memory_space=pltpu.VMEM)
    moved = sum(a.size * a.dtype.itemsize for a in arrays)
    return pl.pallas_call(
        kernel,
        out_shape=[s if hasattr(s, "dtype") else jax.ShapeDtypeStruct(s, F32) for s in shapes],
        in_specs=[pl.BlockSpec(memory_space=pltpu.SMEM)] * len(order) + [where] * len(arrays),
        out_specs=[where] * len(shapes),
        scratch_shapes=list(scratch),
        compiler_params=pltpu.CompilerParams(vmem_limit_bytes=VMEM_LIMIT),
        cost_estimate=pl.CostEstimate(flops=flops, bytes_accessed=moved // 4, transcendentals=0),
    )(*order, *arrays)


def body(
    local_gap,
    previous,
    flexibility,
    schur,
    corner_flex,
    coarse_inverse,
    scaling,
    counts,
    matching,
    corner_map,
):
    gap = local_gap[0, 0]
    prior = previous[0, 0]
    flex = flexibility[0, 0]
    dirichlet = schur[0, 0]
    weights = scaling[0, 0][None, :]
    rows, width = gap.shape
    face = width // 4
    corner_count = corner_flex.shape[2]
    coarse_count = coarse_inverse.shape[1]
    groups = core_groups(lax.axis_size("blk"), lax.axis_size("sector"))
    members = len(groups[0])
    odd_b = lax.rem(lax.axis_index("blk"), 2)
    odd_s = lax.rem(lax.axis_index("sector"), 2)

    chunk = coarse_inverse.shape[0]
    padded = (chunk + 7) // 8 * 8
    coarse_padded = coarse_count // chunk * padded
    own_rows = coarse_inverse.reshape(chunk, coarse_count // chunk, chunk)
    own_rows = jnp.pad(own_rows, ((0, padded - chunk), (0, 0), (0, padded - chunk)))
    own_rows = own_rows.reshape(padded, coarse_padded)
    full_inverse = lax.all_gather(own_rows, "sector", axis=0, tiled=True)

    order = jnp.stack([1 - odd_b, odd_b, 3 - odd_s, 2 + odd_s]).astype(jnp.int32)

    def exchange(links):
        b0, b1, s0, s1 = links
        s1 = swap(s1, "sector", 1)
        s0 = swap(s0, "sector", 0)
        b1 = swap(b1, "blk", 1)
        b0 = swap(b0, "blk", 0)
        return [b0, b1, s0, s1]

    own_map = corner_map[0, 0]
    own_map = (own_map // chunk * padded + lax.rem(own_map, chunk)).astype(F32)
    corners = jnp.pad(corner_flex[0, 0], ((0, SPAN - corner_count), (0, 0)))
    map_rows = jnp.full((8, face), -1.0, F32).at[0, :corner_count].set(own_map)
    came = call(
        first_kernel, [order], [prior, corners, map_rows], [(rows + SPAN + 8, face)] * 4, (), 10**6
    )
    came = exchange(came)

    active = (jnp.arange(face)[None, :] < counts[0, 0][:, None]).astype(F32)
    active_row = active.reshape(1, width)
    (picker,) = call(
        picker_kernel,
        [order],
        [matching[0, 0][None, :], active_row, flex, dirichlet],
        [jax.ShapeDtypeStruct((4, face, face), BF16)],
        (),
        10**8,
    )

    field_shape = (rows, width)
    link_shape = (rows, face)
    sums_shape = (coarse_padded // 2 + 8, LANES)
    square = jax.ShapeDtypeStruct((coarse_padded, coarse_padded), BF16)
    spots_shape = jax.ShapeDtypeStruct((2, coarse_padded, members * PAYLOAD), BF16)
    column_shape = (rows, LANES)
    faces_shape = jax.ShapeDtypeStruct((4, 2 * SPAN, face), BF16)
    taken_shape = jax.ShapeDtypeStruct((5 * SPAN, coarse_padded), BF16)
    big = 2 * rows * width * width
    slow = 8 * 10**9

    def flex_stage(mode, came, field, more):
        out = call(
            functools.partial(flex_kernel, mode),
            [order],
            list(came) + [field, picker, active_row, flex, corners] + more,
            [field_shape, field_shape]
            + [link_shape] * 4
            + [(PAYLOAD, LANES)]
            + [faces_shape, taken_shape] * (mode == 0),
            [pltpu.VMEM((2 * rows if mode == 2 else rows, width), BF16)],
            big,
        )
        return out[0], out[1], out[2:6], *out[6:]

    def gather(payload, links):
        many = jnp.broadcast_to(payload[None], (members, PAYLOAD, LANES))
        many = many.reshape(members * PAYLOAD, LANES)
        got = lax.all_to_all(
            many, BOTH, split_axis=0, concat_axis=0, tiled=True, axis_index_groups=groups
        )
        return got, exchange(links)

    def assemble(mode, *arrays):
        shapes = [sums_shape] + [spots_shape] * (mode == 0)
        kernel = functools.partial(assemble_kernel, mode)
        mine, *more = call(kernel, [], arrays, shapes, (), slow)
        return [mine, swap(mine, "blk", 0)], more

    def solve(mode, sums, *arrays):
        shapes = [(5 * SPAN, LANES)]
        if mode == 0:
            shapes += [square, square]
        if mode == 1:
            shapes += [column_shape, (coarse_padded, LANES), (8, LANES)]
        if mode == 2:
            shapes += [column_shape, column_shape]
        kernel = functools.partial(coarse_kernel, mode)
        return call(kernel, [], [*sums, taken, *arrays], shapes, (), slow)

    def schur_stage(mode, back, came, field, more):
        shapes = [field_shape, field_shape] + [link_shape] * 4
        if mode <= 1:
            shapes += [column_shape]
        if mode >= 1:
            shapes += [field_shape]
        if mode == 1:
            shapes += [field_shape]
        out = call(
            functools.partial(schur_kernel, mode),
            [order],
            [back, *came, field, picker, active_row, corner_faces, dirichlet, weights] + more,
            shapes,
            [pltpu.VMEM((rows, width), BF16)],
            big,
        )
        return out[0], out[1], out[2:6], out[6:]

    extra = jnp.zeros((8, rows), F32).at[3, :corner_count].set(own_map)
    start, field, links, payload, corner_faces, taken = flex_stage(
        0, came, prior, [gap, extra, map_rows]
    )
    got, came = gather(payload, links)
    places = got.reshape(members, PAYLOAD, LANES)[:, 11, rows : rows + corner_count]
    low = places[:, :PAYLOAD].reshape(-1)
    high = jnp.pad(
        places[:, PAYLOAD:], ((0, 0), (0, 2 * PAYLOAD - corner_count)), constant_values=-1.0
    )
    places = jnp.stack([low, high.reshape(-1)]).astype(jnp.int32)
    sums, (spots,) = assemble(0, got, places)
    back, head, rest = solve(0, sums, full_inverse)
    residual, weighted, links, (energy,) = schur_stage(0, back, came, field, [])

    came = exchange(links)
    direction, local, links, payload = flex_stage(1, came, weighted, [energy])
    got, came = gather(payload, links)
    sums, _ = assemble(1, got, spots)
    back, alpha, spread, sums = solve(1, sums, head, rest)
    residual, weighted, links, (energy, multipliers, image) = schur_stage(
        1, back, came, local, [alpha, residual, direction, start]
    )

    came = exchange(links)
    precond, local, links, payload = flex_stage(2, came, weighted, [energy, local])
    got, came = gather(payload, links)
    sums_2, _ = assemble(2, got, spots)
    back, alpha, beta = solve(2, sums_2, head, rest, spread, sums)
    residual, weighted, links, (multipliers,) = schur_stage(
        2, back, came, local, [alpha, residual, precond, multipliers, beta, image, direction]
    )
    came = exchange(links)
    (precond,) = call(
        last_kernel, [order], [*came, weighted, picker, active_row], [field_shape], (), big // 8
    )
    return (multipliers[None, None], residual[None, None], precond[None, None])


def solution(mesh):
    field = P("blk", "sector", None, None)
    vector = P("blk", "sector", None)
    placed = (field, field, field, field, field, P("sector", None), vector, vector, vector, vector)
    return jax.shard_map(
        body,
        mesh=mesh,
        in_specs=placed,
        out_specs=(field, field, field),
        check_vma=False,
    )
```

time: 923 us -> 207 us (0.22); the launches traced: 913 us -> 207 us
  waiting for transfers between devices: 446 us -> 25.5 us
  blocking collectives: 190 us -> 61.1 us
  local copies, waits for them, and re-layouts: 142 us -> 35.6 us
  matrix products: 50.6 us -> 0 us
  Pallas kernels: 0 us -> 31.8 us
  starting transfers between devices: 56.7 us -> 36.9 us
  other arithmetic: 11 us -> 1.53 us
    psum x3 -> x0, waiting for transfers between devices: 386 us -> none  [operator(): total = lax.psum(spread, ('blk', 'sector'))]
    psum x3 -> x0, blocking collectives: 190 us -> none  [the longest x2 127 us: preconditioned(): energy = lax.psum(jnp.sum(residual * precond, axis=1), ('blk', 'sector'))]
    gather x14 -> x0, local copies, waits for them, and re-layouts: 126 us -> none  [pick_rows(): return jnp.take(table, index, axis=0)]
    all_to_all x0 -> x3, blocking collectives: none -> 61.1 us  [gather(): lax.all_to_all(many, BOTH, split_axis=0, concat_axis=0, tiled=True, axis_...]
    dot_general x21 -> x0, matrix products: 50.6 us -> none  [the longest x3 17.9 us: operator(): local = jnp.dot(rounded, flex, preferred_element_type=jnp.float32)]
    pallas_call x0 -> x15, Pallas kernels: none -> 31.8 us  [call(): pl.pallas_call(kernel, out_shape=[s if hasattr(s, 'dtype') else jax.Shape...]
    ppermute x28 -> x31, waiting for transfers between devices: 51 us -> 25.5 us  [swap(): return lax.ppermute(block, axis, route)]
    ppermute x28 -> x31, starting transfers between devices: 56.5 us -> 36.8 us  [swap(): return lax.ppermute(block, axis, route)]
  transfers between devices with their start and end apart: 32 -> 32, of which waited for: 18 -> 13; matrix products, arithmetic and copies ran while one was open for 5% -> 3% of each run, Pallas kernels for 0% -> 6%
where the time goes in v1:
time: 207 us
  blocking collectives  61.1 us (30%)
  starting transfers between devices  36.9 us (18%)
  local copies, waits for them, and re-layouts  35.6 us (17%)
  Pallas kernels  31.8 us (15%)
  waiting for transfers between devices  25.5 us (12%)
  between operations  14.3 us (7%)
    all_to_all x3, blocking collectives, gather(): lax.all_to_all(many, BOTH, split_axis=0, concat_axis=0, tiled=True, axis_...  61.1 us
    ppermute x31, starting transfers between devices, swap(): return lax.ppermute(block, axis, route)  36.8 us
    pallas_call x15, Pallas kernels, call(): pl.pallas_call(kernel, out_shape=[s if hasattr(s, 'dtype') else jax.Shape...  31.8 us
    unnamed x69, local copies, waits for them, and re-layouts  27.9 us
    ppermute x31, waiting for transfers between devices, swap(): return lax.ppermute(block, axis, route)  25.5 us
  transfers between devices with their start and end apart: 32, of which 13 were waited for; matrix products, arithmetic and copies ran while one was open for 3% of the time, Pallas kernels for 6%

profile of v1, /device:TPU:1, one launch (start us, length us, event | category | flops | bytes accessed | tf_op | source)
XLA Modules:
  0.0 206.7 jit_solution(5361734660823067209)
XLA Ops:
  17.3 4.4 %collective-permute-start.3 = (f32[104,512]{1,0:T(8,128)S(1)}, f32[104,512]{1,0:T(8,128)S(1)}, u32[]{:S(2)}, u32[]{:S(2)}) collective-permute-start(f32[104,512]{1,0:T(8,128)S(1)} %get-tuple-element.92), channel_id=1, source_target_pairs={{1,2},{2,1},{3,4},{4,3},{5,6},{6,5},{7,8},{8,7},{9,10},{10,9},{11,... | collective-permute-start | bytes 638984 | tf_op jit(solution)/shard_map/ppermute | solution.py:24
  21.9 3.6 %copy-done = bf16[1,1,2048,2048]{3,2,1,0:T(8,128)(2,1)S(1)} copy-done((bf16[1,1,2048,2048]{3,2,1,0:T(8,128)(2,1)S(1)}, bf16[1,1,2048,2048]{3,2,1,0:T(8,128)(2,1)}, u32[]{:S(2)}) %copy-start) | copy-done | bytes 8388632
  25.5 3.4 %copy-done.2 = bf16[1,1,2048,2048]{3,2,1,0:T(8,128)(2,1)S(1)} copy-done((bf16[1,1,2048,2048]{3,2,1,0:T(8,128)(2,1)S(1)}, bf16[1,1,2048,2048]{3,2,1,0:T(8,128)(2,1)}, u32[]{:S(2)}) %copy-start.2) | copy-done | bytes 8388632
  29.9 2.5 %copy-done.1 = bf16[1,1,2048,2048]{3,2,1,0:T(8,128)(2,1)S(1)} copy-done((bf16[1,1,2048,2048]{3,2,1,0:T(8,128)(2,1)S(1)}, bf16[1,1,2048,2048]{3,2,1,0:T(8,128)(2,1)}, u32[]{:S(2)}) %copy-start.1) | copy-done | bytes 8388632
  32.5 3.7 %shard_map.123 = (f32[64,2048]{1,0:T(8,128)S(1)}, f32[64,2048]{1,0:T(8,128)S(1)}, f32[64,512]{1,0:T(8,128)}, f32[64,512]{1,0:T(8,128)}, f32[64,512]{1,0:T(8,128)...) custom-call(s32[4]{0:T(128)S(1)} %pad_add_fusion.order, ...), custom_call_target="tpu_custom_call" | custom-call | flops 536870912 | bytes 3136000 | tf_op jit(solution)/shard_map/pallas_call | solution.py:305
  37.7 22.6 %all_to_all.24 = f32[64,16,128]{2,1,0:T(8,128)S(1)} all-to-all(f32[64,16,128]{2,1,0:T(8,128)S(1)} %broadcast_in_dim.12), channel_id=1, replica_groups={{0,1,2,3,4,5,6,7,8,9,10,11,12,13,14,15,32,33,34,35,36,37,38,39,40,41,42..., dimensions={0} | all-to-all | bytes 1048576 | tf_op jit(solution)/shard_map/all_to_all | solution.py:408
  67.4 1.8 copy-done.26
  69.2 2.7 %collective-permute-start.4 = (f32[456,128]{1,0:T(8,128)S(1)}, f32[456,128]{1,0:T(8,128)S(1)}, u32[]{:S(2)}, u32[]{:S(2)}) collective-permute-start(f32[456,128]{1,0:T(8,128)S(1)} %get-tuple-element.94.refs_0_), channel_id=1, source_target_pairs={{0,16},{16,0},{32,48},{48,32},{64,80},{80,64},{96,112},{112,96},{1... | collective-permute-start | bytes 700424 | tf_op jit(solution)/shard_map/ppermute | solution.py:24
  75.2 2.1 copy-done.18
  77.2 1.7 copy-done.20
  80.9 1.7 shard_map.125
  88.9 3.0 %shard_map.126 = (f32[64,2048]{1,0:T(8,128)S(1)}, f32[64,2048]{1,0:T(8,128)S(1)}, f32[64,512]{1,0:T(8,128)S(1)}, f32[64,512]{1,0:T(8,128)S(1)}, f32[64,512]{1,0:...) custom-call(s32[4]{0:T(128)S(1)} %pad_add_fusion.order, f32[160,128]{1,0:T(8,128)S(1)} %get-tuple-element.96.refs_0_, ...), custom_call_target="tpu_custom_call" | custom-call | flops 536870912 | bytes 2973696 | tf_op jit(solution)/shard_map/pallas_call | solution.py:305
  94.3 3.6 %collective-permute-start.12 = (f32[64,512]{1,0:T(8,128)S(1)}, f32[64,512]{1,0:T(8,128)S(1)}, u32[]{:S(2)}, u32[]{:S(2)}) collective-permute-start(f32[64,512]{1,0:T(8,128)S(1)} %get-tuple-element.106), channel_id=1, source_target_pairs={{1,2},{2,1},{3,4},{4,3},{5,6},{6,5},{7,8},{8,7},{9,10},{10,9},{11,... | collective-permute-start | bytes 393224 | tf_op jit(solution)/shard_map/ppermute | solution.py:24
  98.4 3.0 %collective-permute-done.12.refs_3_ = f32[64,512]{1,0:T(8,128)S(1)} collective-permute-done((f32[64,512]{1,0:T(8,128)S(1)}, f32[64,512]{1,0:T(8,128)S(1)}, u32[]{:S(2)}, u32[]{:S(2)}) %collective-permute-start.12) | collective-permute-done | bytes 131104 | tf_op jit(solution)/shard_map/ppermute | solution.py:24
  101.4 3.2 %shard_map.127 = (f32[64,2048]{1,0:T(8,128)S(1)}, f32[64,2048]{1,0:T(8,128)S(1)}, f32[64,512]{1,0:T(8,128)S(1)}, f32[64,512]{1,0:T(8,128)S(1)}, f32[64,512]{1,0:...) custom-call(s32[4]{0:T(128)S(1)} %pad_add_fusion.order, f32[64,512]{1,0:T(8,128)S(1)} %collective-permute-done.9.refs_0_, ...), custom_call_target="tpu_custom_call" | custom-call | flops 536870912 | bytes 2926592 | tf_op jit(solution)/shard_map/pallas_call | solution.py:305
  104.7 20.9 %all_to_all.25 = f32[64,16,128]{2,1,0:T(8,128)S(1)} all-to-all(f32[64,16,128]{2,1,0:T(8,128)S(1)} %broadcast_in_dim.13), channel_id=1, replica_groups={{0,1,2,3,4,5,6,7,8,9,10,11,12,13,14,15,32,33,34,35,36,37,38,39,40,41,42..., dimensions={0} | all-to-all | bytes 1048576 | tf_op jit(solution)/shard_map/all_to_all | solution.py:408
  126.9 2.4 %collective-permute-start.13 = (f32[456,128]{1,0:T(8,128)S(1)}, f32[456,128]{1,0:T(8,128)S(1)}, u32[]{:S(2)}, u32[]{:S(2)}) collective-permute-start(f32[456,128]{1,0:T(8,128)S(1)} %shard_map.128.refs_0_), channel_id=1, source_target_pairs={{0,16},{16,0},{32,48},{48,32},{64,80},{80,64},{96,112},{112,96},{1... | collective-permute-start | bytes 700424 | tf_op jit(solution)/shard_map/ppermute | solution.py:24
  134.1 3.0 %collective-permute-done.17.refs_4_ = f32[64,512]{1,0:T(8,128)S(1)} collective-permute-done((f32[64,512]{1,0:T(8,128)S(1)}, f32[64,512]{1,0:T(8,128)S(1)}, u32[]{:S(2)}, u32[]{:S(2)}) %collective-permute-start.17) | collective-permute-done | bytes 131104 | tf_op jit(solution)/shard_map/ppermute | solution.py:24
  137.1 3.1 %shard_map.130 = (f32[64,2048]{1,0:T(8,128)S(1)}, f32[64,2048]{1,0:T(8,128)S(1)}, f32[64,512]{1,0:T(8,128)S(1)}, f32[64,512]{1,0:T(8,128)S(1)}, f32[64,512]{1,0:...) custom-call(s32[4]{0:T(128)S(1)} %pad_add_fusion.order, ...), custom_call_target="tpu_custom_call" | custom-call | flops 536870912 | bytes 3375104 | tf_op jit(solution)/shard_map/pallas_call | solution.py:305
  140.1 2.2 %collective-permute-start.18 = (f32[64,512]{1,0:T(8,128)S(1)}, f32[64,512]{1,0:T(8,128)S(1)}, u32[]{:S(2)}, u32[]{:S(2)}) collective-permute-start(f32[64,512]{1,0:T(8,128)S(1)} %get-tuple-element.123), channel_id=1, source_target_pairs={{0,16},{16,0},{32,48},{48,32},{64,80},{80,64},{96,112},{112,96},{1... | collective-permute-start | bytes 393224 | tf_op jit(solution)/shard_map/ppermute | solution.py:24
  144.4 2.7 %collective-permute-done.19.refs_1_ = f32[64,512]{1,0:T(8,128)S(1)} collective-permute-done((f32[64,512]{1,0:T(8,128)S(1)}, f32[64,512]{1,0:T(8,128)S(1)}, u32[]{:S(2)}, u32[]{:S(2)}) %collective-permute-start.19) | collective-permute-done | bytes 131104 | tf_op jit(solution)/shard_map/ppermute | solution.py:24
  148.0 3.3 %collective-permute-done.21.refs_3_ = f32[64,512]{1,0:T(8,128)S(1)} collective-permute-done((f32[64,512]{1,0:T(8,128)S(1)}, f32[64,512]{1,0:T(8,128)S(1)}, u32[]{:S(2)}, u32[]{:S(2)}) %collective-permute-start.21) | collective-permute-done | bytes 131104 | tf_op jit(solution)/shard_map/ppermute | solution.py:24
  151.3 3.1 %shard_map.131 = (f32[64,2048]{1,0:T(8,128)S(1)}, f32[64,2048]{1,0:T(8,128)S(1)}, f32[64,512]{1,0:T(8,128)S(1)}, f32[64,512]{1,0:T(8,128)S(1)}, f32[64,512]{1,0:...) custom-call(s32[4]{0:T(128)S(1)} %pad_add_fusion.order, f32[64,512]{1,0:T(8,128)S(1)} %collective-permute-done.18.refs_0_, ...), custom_call_target="tpu_custom_call" | custom-call | flops 536870912 | bytes 3057664 | tf_op jit(solution)/shard_map/pallas_call | solution.py:305
  154.4 17.6 %all_to_all.26 = f32[64,16,128]{2,1,0:T(8,128)S(1)} all-to-all(f32[64,16,128]{2,1,0:T(8,128)S(1)} %broadcast_in_dim.14), channel_id=1, replica_groups={{0,1,2,3,4,5,6,7,8,9,10,11,12,13,14,15,32,33,34,35,36,37,38,39,40,41,42..., dimensions={0} | all-to-all | bytes 1048576 | tf_op jit(solution)/shard_map/all_to_all | solution.py:408
  173.3 2.4 %collective-permute-start.22 = (f32[456,128]{1,0:T(8,128)S(1)}, f32[456,128]{1,0:T(8,128)S(1)}, u32[]{:S(2)}, u32[]{:S(2)}) collective-permute-start(f32[456,128]{1,0:T(8,128)S(1)} %shard_map.132.refs_0_), channel_id=1, source_target_pairs={{0,16},{16,0},{32,48},{48,32},{64,80},{80,64},{96,112},{112,96},{1... | collective-permute-start | bytes 700424 | tf_op jit(solution)/shard_map/ppermute | solution.py:24
  177.8 1.7 shard_map.133
  180.5 3.0 %collective-permute-done.26.refs_4_ = f32[64,512]{1,0:T(8,128)S(1)} collective-permute-done((f32[64,512]{1,0:T(8,128)S(1)}, f32[64,512]{1,0:T(8,128)S(1)}, u32[]{:S(2)}, u32[]{:S(2)}) %collective-permute-start.26) | collective-permute-done | bytes 131104 | tf_op jit(solution)/shard_map/ppermute | solution.py:24
  183.5 3.5 %shard_map.134 = (f32[64,2048]{1,0:T(8,128)}, f32[64,2048]{1,0:T(8,128)S(1)}, f32[64,512]{1,0:T(8,128)S(1)}, f32[64,512]{1,0:T(8,128)S(1)}, f32[64,512]{1,0:T(8,...) custom-call(s32[4]{0:T(128)S(1)} %pad_add_fusion.order, f32[160,128]{1,0:T(8,128)S(1)} %get-tuple-element.132.refs_0_, ...), custom_call_target="tpu_custom_call" | custom-call | flops 536870912 | bytes 3645440 | tf_op jit(solution)/shard_map/pallas_call | solution.py:305
  187.0 2.2 %collective-permute-start.27 = (f32[64,512]{1,0:T(8,128)S(1)}, f32[64,512]{1,0:T(8,128)S(1)}, u32[]{:S(2)}, u32[]{:S(2)}) collective-permute-start(f32[64,512]{1,0:T(8,128)S(1)} %get-tuple-element.146), channel_id=1, source_target_pairs={{0,16},{16,0},{32,48},{48,32},{64,80},{80,64},{96,112},{112,96},{1... | collective-permute-start | bytes 393224 | tf_op jit(solution)/shard_map/ppermute | solution.py:24
  191.0 2.8 %collective-permute-done.28.refs_1_ = f32[64,512]{1,0:T(8,128)S(1)} collective-permute-done((f32[64,512]{1,0:T(8,128)S(1)}, f32[64,512]{1,0:T(8,128)S(1)}, u32[]{:S(2)}, u32[]{:S(2)}) %collective-permute-start.28) | collective-permute-done | bytes 131104 | tf_op jit(solution)/shard_map/ppermute | solution.py:24
  194.6 3.3 %collective-permute-done.30.refs_3_ = f32[64,512]{1,0:T(8,128)S(1)} collective-permute-done((f32[64,512]{1,0:T(8,128)S(1)}, f32[64,512]{1,0:T(8,128)S(1)}, u32[]{:S(2)}, u32[]{:S(2)}) %collective-permute-start.30) | collective-permute-done | bytes 131104 | tf_op jit(solution)/shard_map/ppermute | solution.py:24
  198.0 1.9 shard_map.135
  (140 shorter events, 50.4 us)
Async XLA Ops:
  7.2 68.0 %all-gather.2.cloned.1.call-start = ((), (), s32[]{:S(2)}) async-start(), calls=%async_computation.3 | async-start | bytes 3411968 | tf_op jit(solution)/shard_map/all_gather | solution.py:348
  12.8 17.0 %collective-permute-start = (f32[104,512]{1,0:T(8,128)S(1)}, f32[104,512]{1,0:T(8,128)S(1)}, u32[]{:S(2)}, u32[]{:S(2)}) collective-permute-start(f32[104,512]{1,0:T(8,128)S(1)} %get-tuple-element.89), channel_id=1, source_target_pairs={{0,16},{16,0},{32,48},{48,32},{64,80},{80,64},{96,112},{112,96},{1... | collective-permute-start | bytes 638984 | tf_op jit(solution)/shard_map/ppermute | solution.py:24
  14.3 15.5 %collective-permute-start.1 = (f32[104,512]{1,0:T(8,128)S(1)}, f32[104,512]{1,0:T(8,128)S(1)}, u32[]{:S(2)}, u32[]{:S(2)}) collective-permute-start(f32[104,512]{1,0:T(8,128)S(1)} %get-tuple-element.90), channel_id=1, source_target_pairs={{16,32},{32,16},{48,64},{64,48},{80,96},{96,80},{112,0},{0,112},{1... | collective-permute-start | bytes 638984 | tf_op jit(solution)/shard_map/ppermute | solution.py:24
  15.7 14.1 %collective-permute-start.2 = (f32[104,512]{1,0:T(8,128)S(1)}, f32[104,512]{1,0:T(8,128)S(1)}, u32[]{:S(2)}, u32[]{:S(2)}) collective-permute-start(f32[104,512]{1,0:T(8,128)S(1)} %get-tuple-element.91), channel_id=1, source_target_pairs={{0,1},{1,0},{2,3},{3,2},{4,5},{5,4},{6,7},{7,6},{8,9},{9,8},{10,11... | collective-permute-start | bytes 638984 | tf_op jit(solution)/shard_map/ppermute | solution.py:24
  17.3 12.5 %collective-permute-start.3 = (f32[104,512]{1,0:T(8,128)S(1)}, f32[104,512]{1,0:T(8,128)S(1)}, u32[]{:S(2)}, u32[]{:S(2)}) collective-permute-start(f32[104,512]{1,0:T(8,128)S(1)} %get-tuple-element.92), channel_id=1, source_target_pairs={{1,2},{2,1},{3,4},{4,3},{5,6},{6,5},{7,8},{8,7},{9,10},{10,9},{11,... | collective-permute-start | bytes 638984 | tf_op jit(solution)/shard_map/ppermute | solution.py:24
  69.2 5.3 %collective-permute-start.4 = (f32[456,128]{1,0:T(8,128)S(1)}, f32[456,128]{1,0:T(8,128)S(1)}, u32[]{:S(2)}, u32[]{:S(2)}) collective-permute-start(f32[456,128]{1,0:T(8,128)S(1)} %get-tuple-element.94.refs_0_), channel_id=1, source_target_pairs={{0,16},{16,0},{32,48},{48,32},{64,80},{80,64},{96,112},{112,96},{1... | collective-permute-start | bytes 700424 | tf_op jit(solution)/shard_map/ppermute | solution.py:24
  72.6 10.0 %collective-permute-start.5 = (f32[64,512]{1,0:T(8,128)}, f32[64,512]{1,0:T(8,128)S(1)}, u32[]{:S(2)}, u32[]{:S(2)}) collective-permute-start(f32[64,512]{1,0:T(8,128)} %get-tuple-element.97), channel_id=1, source_target_pairs={{0,16},{16,0},{32,48},{48,32},{64,80},{80,64},{96,112},{112,96},{1... | collective-permute-start | bytes 393224 | tf_op jit(solution)/shard_map/ppermute | solution.py:24
  72.6 10.7 %collective-permute-start.6 = (f32[64,512]{1,0:T(8,128)}, f32[64,512]{1,0:T(8,128)S(1)}, u32[]{:S(2)}, u32[]{:S(2)}) collective-permute-start(f32[64,512]{1,0:T(8,128)} %get-tuple-element.98), channel_id=1, source_target_pairs={{16,32},{32,16},{48,64},{64,48},{80,96},{96,80},{112,0},{0,112},{1... | collective-permute-start | bytes 393224 | tf_op jit(solution)/shard_map/ppermute | solution.py:24
  72.6 11.3 %collective-permute-start.7 = (f32[64,512]{1,0:T(8,128)}, f32[64,512]{1,0:T(8,128)S(1)}, u32[]{:S(2)}, u32[]{:S(2)}) collective-permute-start(f32[64,512]{1,0:T(8,128)} %get-tuple-element.99), channel_id=1, source_target_pairs={{0,1},{1,0},{2,3},{3,2},{4,5},{5,4},{6,7},{7,6},{8,9},{9,8},{10,11... | collective-permute-start | bytes 393224 | tf_op jit(solution)/shard_map/ppermute | solution.py:24
  73.1 11.5 %collective-permute-start.8 = (f32[64,512]{1,0:T(8,128)}, f32[64,512]{1,0:T(8,128)S(1)}, u32[]{:S(2)}, u32[]{:S(2)}) collective-permute-start(f32[64,512]{1,0:T(8,128)} %get-tuple-element.100), channel_id=1, source_target_pairs={{1,2},{2,1},{3,4},{4,3},{5,6},{6,5},{7,8},{8,7},{9,10},{10,9},{11,... | collective-permute-start | bytes 393224 | tf_op jit(solution)/shard_map/ppermute | solution.py:24
  91.8 6.1 %collective-permute-start.9 = (f32[64,512]{1,0:T(8,128)S(1)}, f32[64,512]{1,0:T(8,128)S(1)}, u32[]{:S(2)}, u32[]{:S(2)}) collective-permute-start(f32[64,512]{1,0:T(8,128)S(1)} %get-tuple-element.103), channel_id=1, source_target_pairs={{0,16},{16,0},{32,48},{48,32},{64,80},{80,64},{96,112},{112,96},{1... | collective-permute-start | bytes 393224 | tf_op jit(solution)/shard_map/ppermute | solution.py:24
  93.3 4.7 %collective-permute-start.10 = (f32[64,512]{1,0:T(8,128)S(1)}, f32[64,512]{1,0:T(8,128)S(1)}, u32[]{:S(2)}, u32[]{:S(2)}) collective-permute-start(f32[64,512]{1,0:T(8,128)S(1)} %get-tuple-element.104), channel_id=1, source_target_pairs={{16,32},{32,16},{48,64},{64,48},{80,96},{96,80},{112,0},{0,112},{1... | collective-permute-start | bytes 393224 | tf_op jit(solution)/shard_map/ppermute | solution.py:24
  94.3 4.1 %collective-permute-start.11 = (f32[64,512]{1,0:T(8,128)S(1)}, f32[64,512]{1,0:T(8,128)S(1)}, u32[]{:S(2)}, u32[]{:S(2)}) collective-permute-start(f32[64,512]{1,0:T(8,128)S(1)} %get-tuple-element.105), channel_id=1, source_target_pairs={{0,1},{1,0},{2,3},{3,2},{4,5},{5,4},{6,7},{7,6},{8,9},{9,8},{10,11... | collective-permute-start | bytes 393224 | tf_op jit(solution)/shard_map/ppermute | solution.py:24
  94.3 7.1 %collective-permute-start.12 = (f32[64,512]{1,0:T(8,128)S(1)}, f32[64,512]{1,0:T(8,128)S(1)}, u32[]{:S(2)}, u32[]{:S(2)}) collective-permute-start(f32[64,512]{1,0:T(8,128)S(1)} %get-tuple-element.106), channel_id=1, source_target_pairs={{1,2},{2,1},{3,4},{4,3},{5,6},{6,5},{7,8},{8,7},{9,10},{10,9},{11,... | collective-permute-start | bytes 393224 | tf_op jit(solution)/shard_map/ppermute | solution.py:24
  126.9 4.5 %collective-permute-start.13 = (f32[456,128]{1,0:T(8,128)S(1)}, f32[456,128]{1,0:T(8,128)S(1)}, u32[]{:S(2)}, u32[]{:S(2)}) collective-permute-start(f32[456,128]{1,0:T(8,128)S(1)} %shard_map.128.refs_0_), channel_id=1, source_target_pairs={{0,16},{16,0},{32,48},{48,32},{64,80},{80,64},{96,112},{112,96},{1... | collective-permute-start | bytes 700424 | tf_op jit(solution)/shard_map/ppermute | solution.py:24
  129.3 3.7 %collective-permute-start.14 = (f32[64,512]{1,0:T(8,128)S(1)}, f32[64,512]{1,0:T(8,128)S(1)}, u32[]{:S(2)}, u32[]{:S(2)}) collective-permute-start(f32[64,512]{1,0:T(8,128)S(1)} %get-tuple-element.114), channel_id=1, source_target_pairs={{0,16},{16,0},{32,48},{48,32},{64,80},{80,64},{96,112},{112,96},{1... | collective-permute-start | bytes 393224 | tf_op jit(solution)/shard_map/ppermute | solution.py:24
  129.4 4.7 %collective-permute-start.15 = (f32[64,512]{1,0:T(8,128)S(1)}, f32[64,512]{1,0:T(8,128)S(1)}, u32[]{:S(2)}, u32[]{:S(2)}) collective-permute-start(f32[64,512]{1,0:T(8,128)S(1)} %get-tuple-element.115), channel_id=1, source_target_pairs={{16,32},{32,16},{48,64},{64,48},{80,96},{96,80},{112,0},{0,112},{1... | collective-permute-start | bytes 393224 | tf_op jit(solution)/shard_map/ppermute | solution.py:24
  129.6 4.5 %collective-permute-start.16 = (f32[64,512]{1,0:T(8,128)S(1)}, f32[64,512]{1,0:T(8,128)S(1)}, u32[]{:S(2)}, u32[]{:S(2)}) collective-permute-start(f32[64,512]{1,0:T(8,128)S(1)} %get-tuple-element.116), channel_id=1, source_target_pairs={{0,1},{1,0},{2,3},{3,2},{4,5},{5,4},{6,7},{7,6},{8,9},{9,8},{10,11... | collective-permute-start | bytes 393224 | tf_op jit(solution)/shard_map/ppermute | solution.py:24
  129.9 7.1 %collective-permute-start.17 = (f32[64,512]{1,0:T(8,128)S(1)}, f32[64,512]{1,0:T(8,128)S(1)}, u32[]{:S(2)}, u32[]{:S(2)}) collective-permute-start(f32[64,512]{1,0:T(8,128)S(1)} %get-tuple-element.117), channel_id=1, source_target_pairs={{1,2},{2,1},{3,4},{4,3},{5,6},{6,5},{7,8},{8,7},{9,10},{10,9},{11,... | collective-permute-start | bytes 393224 | tf_op jit(solution)/shard_map/ppermute | solution.py:24
  140.1 4.2 %collective-permute-start.18 = (f32[64,512]{1,0:T(8,128)S(1)}, f32[64,512]{1,0:T(8,128)S(1)}, u32[]{:S(2)}, u32[]{:S(2)}) collective-permute-start(f32[64,512]{1,0:T(8,128)S(1)} %get-tuple-element.123), channel_id=1, source_target_pairs={{0,16},{16,0},{32,48},{48,32},{64,80},{80,64},{96,112},{112,96},{1... | collective-permute-start | bytes 393224 | tf_op jit(solution)/shard_map/ppermute | solution.py:24
  142.4 4.7 %collective-permute-start.19 = (f32[64,512]{1,0:T(8,128)S(1)}, f32[64,512]{1,0:T(8,128)S(1)}, u32[]{:S(2)}, u32[]{:S(2)}) collective-permute-start(f32[64,512]{1,0:T(8,128)S(1)} %get-tuple-element.124), channel_id=1, source_target_pairs={{16,32},{32,16},{48,64},{64,48},{80,96},{96,80},{112,0},{0,112},{1... | collective-permute-start | bytes 393224 | tf_op jit(solution)/shard_map/ppermute | solution.py:24
  143.3 4.7 %collective-permute-start.20 = (f32[64,512]{1,0:T(8,128)S(1)}, f32[64,512]{1,0:T(8,128)S(1)}, u32[]{:S(2)}, u32[]{:S(2)}) collective-permute-start(f32[64,512]{1,0:T(8,128)S(1)} %get-tuple-element.125), channel_id=1, source_target_pairs={{0,1},{1,0},{2,3},{3,2},{4,5},{5,4},{6,7},{7,6},{8,9},{9,8},{10,11... | collective-permute-start | bytes 393224 | tf_op jit(solution)/shard_map/ppermute | solution.py:24
  143.3 8.0 %collective-permute-start.21 = (f32[64,512]{1,0:T(8,128)S(1)}, f32[64,512]{1,0:T(8,128)S(1)}, u32[]{:S(2)}, u32[]{:S(2)}) collective-permute-start(f32[64,512]{1,0:T(8,128)S(1)} %get-tuple-element.126), channel_id=1, source_target_pairs={{1,2},{2,1},{3,4},{4,3},{5,6},{6,5},{7,8},{8,7},{9,10},{10,9},{11,... | collective-permute-start | bytes 393224 | tf_op jit(solution)/shard_map/ppermute | solution.py:24
  173.3 4.5 %collective-permute-start.22 = (f32[456,128]{1,0:T(8,128)S(1)}, f32[456,128]{1,0:T(8,128)S(1)}, u32[]{:S(2)}, u32[]{:S(2)}) collective-permute-start(f32[456,128]{1,0:T(8,128)S(1)} %shard_map.132.refs_0_), channel_id=1, source_target_pairs={{0,16},{16,0},{32,48},{48,32},{64,80},{80,64},{96,112},{112,96},{1... | collective-permute-start | bytes 700424 | tf_op jit(solution)/shard_map/ppermute | solution.py:24
  175.7 3.8 %collective-permute-start.23 = (f32[64,512]{1,0:T(8,128)S(1)}, f32[64,512]{1,0:T(8,128)S(1)}, u32[]{:S(2)}, u32[]{:S(2)}) collective-permute-start(f32[64,512]{1,0:T(8,128)S(1)} %get-tuple-element.133), channel_id=1, source_target_pairs={{0,16},{16,0},{32,48},{48,32},{64,80},{80,64},{96,112},{112,96},{1... | collective-permute-start | bytes 393224 | tf_op jit(solution)/shard_map/ppermute | solution.py:24
  175.8 4.7 %collective-permute-start.24 = (f32[64,512]{1,0:T(8,128)S(1)}, f32[64,512]{1,0:T(8,128)S(1)}, u32[]{:S(2)}, u32[]{:S(2)}) collective-permute-start(f32[64,512]{1,0:T(8,128)S(1)} %get-tuple-element.134), channel_id=1, source_target_pairs={{16,32},{32,16},{48,64},{64,48},{80,96},{96,80},{112,0},{0,112},{1... | collective-permute-start | bytes 393224 | tf_op jit(solution)/shard_map/ppermute | solution.py:24
  176.0 4.5 %collective-permute-start.25 = (f32[64,512]{1,0:T(8,128)S(1)}, f32[64,512]{1,0:T(8,128)S(1)}, u32[]{:S(2)}, u32[]{:S(2)}) collective-permute-start(f32[64,512]{1,0:T(8,128)S(1)} %get-tuple-element.135), channel_id=1, source_target_pairs={{0,1},{1,0},{2,3},{3,2},{4,5},{5,4},{6,7},{7,6},{8,9},{9,8},{10,11... | collective-permute-start | bytes 393224 | tf_op jit(solution)/shard_map/ppermute | solution.py:24
  176.3 7.1 %collective-permute-start.26 = (f32[64,512]{1,0:T(8,128)S(1)}, f32[64,512]{1,0:T(8,128)S(1)}, u32[]{:S(2)}, u32[]{:S(2)}) collective-permute-start(f32[64,512]{1,0:T(8,128)S(1)} %get-tuple-element.136), channel_id=1, source_target_pairs={{1,2},{2,1},{3,4},{4,3},{5,6},{6,5},{7,8},{8,7},{9,10},{10,9},{11,... | collective-permute-start | bytes 393224 | tf_op jit(solution)/shard_map/ppermute | solution.py:24
  187.0 4.1 %collective-permute-start.27 = (f32[64,512]{1,0:T(8,128)S(1)}, f32[64,512]{1,0:T(8,128)S(1)}, u32[]{:S(2)}, u32[]{:S(2)}) collective-permute-start(f32[64,512]{1,0:T(8,128)S(1)} %get-tuple-element.146), channel_id=1, source_target_pairs={{0,16},{16,0},{32,48},{48,32},{64,80},{80,64},{96,112},{112,96},{1... | collective-permute-start | bytes 393224 | tf_op jit(solution)/shard_map/ppermute | solution.py:24
  189.1 4.7 %collective-permute-start.28 = (f32[64,512]{1,0:T(8,128)S(1)}, f32[64,512]{1,0:T(8,128)S(1)}, u32[]{:S(2)}, u32[]{:S(2)}) collective-permute-start(f32[64,512]{1,0:T(8,128)S(1)} %get-tuple-element.147), channel_id=1, source_target_pairs={{16,32},{32,16},{48,64},{64,48},{80,96},{96,80},{112,0},{0,112},{1... | collective-permute-start | bytes 393224 | tf_op jit(solution)/shard_map/ppermute | solution.py:24
  190.0 4.7 %collective-permute-start.29 = (f32[64,512]{1,0:T(8,128)S(1)}, f32[64,512]{1,0:T(8,128)S(1)}, u32[]{:S(2)}, u32[]{:S(2)}) collective-permute-start(f32[64,512]{1,0:T(8,128)S(1)} %get-tuple-element.148), channel_id=1, source_target_pairs={{0,1},{1,0},{2,3},{3,2},{4,5},{5,4},{6,7},{7,6},{8,9},{9,8},{10,11... | collective-permute-start | bytes 393224 | tf_op jit(solution)/shard_map/ppermute | solution.py:24
  190.0 8.0 %collective-permute-start.30 = (f32[64,512]{1,0:T(8,128)S(1)}, f32[64,512]{1,0:T(8,128)S(1)}, u32[]{:S(2)}, u32[]{:S(2)}) collective-permute-start(f32[64,512]{1,0:T(8,128)S(1)} %get-tuple-element.149), channel_id=1, source_target_pairs={{1,2},{2,1},{3,4},{4,3},{5,6},{6,5},{7,8},{8,7},{9,10},{10,9},{11,... | collective-permute-start | bytes 393224 | tf_op jit(solution)/shard_map/ppermute | solution.py:24
  (34 other events, 166.4 us)
Sparse Core Ops, SparseCore 0:
  10.2 56.1 all-gather.1

commit v2 on v1

--- a/solution.py
+++ b/solution.py
@@ -9,6 +9,7 @@
 
 BOTH = ("blk", "sector")
 PAYLOAD = 16
+MAP_ROW = 11
 LANES = 128
 SPAN = 32
 F32, BF16 = jnp.float32, jnp.bfloat16
@@ -76,7 +77,7 @@
     came = [refs.pop(0) for _ in range(4)]
     field, picker, active, flex, corners = [refs.pop(0) for _ in range(5)]
     if mode == 0:
-        gap, extra, numbers = refs.pop(0), refs.pop(0), refs.pop(0)
+        gap, numbers = refs.pop(0), refs.pop(0)
     if mode >= 1:
         energy = refs.pop(0)
     if mode == 2:
@@ -131,7 +132,8 @@
     payload[0:16, 0:rows] = part[0:16]
     payload[0:8, rows : 2 * rows] = part[16:24]
     if mode == 0:
-        scalars = extra[...]
+        at = lax.broadcasted_iota(jnp.int32, (8, rows), 0)
+        scalars = jnp.where(at == MAP_ROW - 8, numbers[0:1, 0:rows], 0.0)
     else:
         lane = lax.broadcasted_iota(jnp.int32, (rows, LANES), 1)
         table = jnp.where(lane == 0, energy[...], jnp.where(lane == 1, inner, 0.0))
@@ -140,7 +142,11 @@
     payload[8:16, rows : 2 * rows] = scalars
 
 
-def first_kernel(order, prior, corners, numbers, *links):
+def first_kernel(order, prior, corner_flex, numbers, corners, *links):
+    count, width = corner_flex.shape
+    blank = jnp.zeros((SPAN - count, width), F32)
+    full = jnp.concatenate([corner_flex[...].astype(F32), blank], axis=0)
+    corners[...] = full.astype(BF16)
     rows, width = prior.shape
     face = width // 4
     for link in range(4):
@@ -161,18 +167,29 @@
 
 def assemble_kernel(mode, *refs):
     if mode == 0:
-        got, places, out, spots = refs[0], refs[1], refs[-2], refs[-1]
-        count = spots.shape[1]
-        source = lax.broadcasted_iota(jnp.int32, (LANES, got.shape[0]), 0)
+        got, out, spots = refs
+        members, count = got.shape[0] // PAYLOAD, got.shape[0]
+        maps = pltpu.roll(got[pl.ds(MAP_ROW, members, stride=PAYLOAD), :], LANES // 2, 1)
+        maps = jnp.concatenate(parts_of(maps, 2), axis=0)
+        lane = lax.broadcasted_iota(jnp.int32, (LANES, count), 0)
+        slot = lax.broadcasted_iota(jnp.int32, (LANES, count), 1) & (PAYLOAD - 1)
+        member = lax.broadcasted_iota(jnp.int32, (members, count), 0) * PAYLOAD
+        gap = lax.broadcasted_iota(jnp.int32, (members, count), 1) - member
+        own = (gap >= 0) & (gap < PAYLOAD)
+        source = lax.broadcasted_iota(jnp.int32, (LANES, count), 0).astype(F32)
         for which in range(2):
-            for at in range(0, count, LANES):
-                hit = source + at == places[which : which + 1, :]
-                spots[which, at : at + LANES, :] = jnp.where(hit, 1.0, 0.0).astype(BF16)
+            pickup = jnp.where(lane == slot + which * PAYLOAD, 1.0, 0.0).astype(BF16)
+            number = dot(maps, pickup)
+            number = jnp.where(own, number[:members] + number[members:], 0.0)
+            number = jnp.sum(number, axis=0, keepdims=True)
+            for at in range(0, spots.shape[1], LANES):
+                hit = jnp.where(source + float(at) == number, 1.0, 0.0)
+                spots[which, at : at + LANES, :] = hit.astype(BF16)
     else:
-        got, spots, out = refs[0], refs[1], refs[-1]
+        got, spots, out = refs
     members = got.shape[0] // PAYLOAD
     half = spots.shape[1] // 2
-    both = jnp.concatenate(parts_of(got[...], 2), axis=1)
+    both = jnp.concatenate(parts_of(got[:, 0:LANES], 2), axis=1)
     low = dot(spots[0], both)
     high = dot(spots[1], both)
     low = low[:, :LANES] + low[:, LANES:]
@@ -182,7 +199,7 @@
     out[0:half, :] = jnp.where(
         lane < LANES // 2, spread[:half], pltpu.roll(spread[half:], LANES // 2, 1)
     )
-    total = jnp.sum(got[...].reshape(members, PAYLOAD, LANES), axis=0)
+    total = jnp.sum(got[:, 0:LANES].reshape(members, PAYLOAD, LANES), axis=0)
     out[half : half + 8, :] = total[8:16]
 
 
@@ -359,12 +376,16 @@
 
     own_map = corner_map[0, 0]
     own_map = (own_map // chunk * padded + lax.rem(own_map, chunk)).astype(F32)
-    corners = jnp.pad(corner_flex[0, 0], ((0, SPAN - corner_count), (0, 0)))
     map_rows = jnp.full((8, face), -1.0, F32).at[0, :corner_count].set(own_map)
-    came = call(
-        first_kernel, [order], [prior, corners, map_rows], [(rows + SPAN + 8, face)] * 4, (), 10**6
-    )
-    came = exchange(came)
+    corners, *links = call(
+        first_kernel,
+        [order],
+        [prior, corner_flex[0, 0], map_rows],
+        [jax.ShapeDtypeStruct((SPAN, width), BF16)] + [(rows + SPAN + 8, face)] * 4,
+        (),
+        10**6,
+    )
+    came = exchange(links)
 
     active = (jnp.arange(face)[None, :] < counts[0, 0][:, None]).astype(F32)
     active_row = active.reshape(1, width)
@@ -403,8 +424,8 @@
         return out[0], out[1], out[2:6], *out[6:]
 
     def gather(payload, links):
-        many = jnp.broadcast_to(payload[None], (members, PAYLOAD, LANES))
-        many = many.reshape(members * PAYLOAD, LANES)
+        many = jnp.broadcast_to(payload[None], (members,) + payload.shape)
+        many = many.reshape(members * PAYLOAD, payload.shape[1])
         got = lax.all_to_all(
             many, BOTH, split_axis=0, concat_axis=0, tiled=True, axis_index_groups=groups
         )
@@ -445,18 +466,11 @@
         )
         return out[0], out[1], out[2:6], out[6:]
 
-    extra = jnp.zeros((8, rows), F32).at[3, :corner_count].set(own_map)
     start, field, links, payload, corner_faces, taken = flex_stage(
-        0, came, prior, [gap, extra, map_rows]
+        0, came, prior, [gap, map_rows]
     )
     got, came = gather(payload, links)
-    places = got.reshape(members, PAYLOAD, LANES)[:, 11, rows : rows + corner_count]
-    low = places[:, :PAYLOAD].reshape(-1)
-    high = jnp.pad(
-        places[:, PAYLOAD:], ((0, 0), (0, 2 * PAYLOAD - corner_count)), constant_values=-1.0
-    )
-    places = jnp.stack([low, high.reshape(-1)]).astype(jnp.int32)
-    sums, (spots,) = assemble(0, got, places)
+    sums, (spots,) = assemble(0, got)
     back, head, rest = solve(0, sums, full_inverse)
     residual, weighted, links, (energy,) = schur_stage(0, back, came, field, [])
 

time: 207 us -> 197 us (0.952)
  local copies, waits for them, and re-layouts: 35.6 us -> 23.9 us
    unnamed x69 -> x47, local copies, waits for them, and re-layouts: 27.9 us -> 21.6 us
    pad x2 -> x0, local copies, waits for them, and re-layouts: 2.28 us -> none  [the longest x1 1.38 us: body(): jnp.pad(places[:, PAYLOAD:], ((0, 0), (0, 2 * PAYLOAD - corner_count)), c...]
    another operation x2 -> x0, local copies, waits for them, and re-layouts: 2.27 us -> none  [body(): places = jnp.stack([low, high.reshape(-1)]).astype(jnp.int32)]
  transfers between devices with their start and end apart: 32 -> 32, of which waited for: 13 -> 12; matrix products, arithmetic and copies ran while one was open for 3% -> 1% of each run, Pallas kernels for 6% -> 6%
where the time goes in v2:
time: 197 us
  blocking collectives  61 us (31%)
  starting transfers between devices  36.9 us (19%)
  Pallas kernels  33.4 us (17%)
  waiting for transfers between devices  25.5 us (13%)
  local copies, waits for them, and re-layouts  23.9 us (12%)
  between operations  14.3 us (7%)
    all_to_all x3, blocking collectives, gather(): lax.all_to_all(many, BOTH, split_axis=0, concat_axis=0, tiled=True, axis_...  61 us
    ppermute x31, starting transfers between devices, swap(): return lax.ppermute(block, axis, route)  36.9 us
    pallas_call x15, Pallas kernels, call(): pl.pallas_call(kernel, out_shape=[s if hasattr(s, 'dtype') else jax.Shape...  33.4 us
    ppermute x31, waiting for transfers between devices, swap(): return lax.ppermute(block, axis, route)  25.4 us
    unnamed x47, local copies, waits for them, and re-layouts  21.6 us
  transfers between devices with their start and end apart: 32, of which 12 were waited for; matrix products, arithmetic and copies ran while one was open for 1% of the time, Pallas kernels for 6%

profile of v2, /device:TPU:1, one launch (start us, length us, event | category | flops | bytes accessed | tf_op | source)
XLA Modules:
  0.0 196.5 jit_solution(1360474274953734252)
XLA Ops:
  17.3 4.4 %collective-permute-start.3 = (f32[104,512]{1,0:T(8,128)S(1)}, f32[104,512]{1,0:T(8,128)S(1)}, u32[]{:S(2)}, u32[]{:S(2)}) collective-permute-start(f32[104,512]{1,0:T(8,128)S(1)} %get-tuple-element.81), channel_id=1, source_target_pairs={{1,2},{2,1},{3,4},{4,3},{5,6},{6,5},{7,8},{8,7},{9,10},{10,9},{11,... | collective-permute-start | bytes 638984 | tf_op jit(solution)/shard_map/ppermute | solution.py:25
  22.5 3.5 %copy-done = bf16[1,1,2048,2048]{3,2,1,0:T(8,128)(2,1)S(1)} copy-done((bf16[1,1,2048,2048]{3,2,1,0:T(8,128)(2,1)S(1)}, bf16[1,1,2048,2048]{3,2,1,0:T(8,128)(2,1)}, u32[]{:S(2)}) %copy-start) | copy-done | bytes 8388632
  26.0 3.4 %copy-done.2 = bf16[1,1,2048,2048]{3,2,1,0:T(8,128)(2,1)S(1)} copy-done((bf16[1,1,2048,2048]{3,2,1,0:T(8,128)(2,1)S(1)}, bf16[1,1,2048,2048]{3,2,1,0:T(8,128)(2,1)}, u32[]{:S(2)}) %copy-start.2) | copy-done | bytes 8388632
  31.1 2.4 %copy-done.1 = bf16[1,1,2048,2048]{3,2,1,0:T(8,128)(2,1)S(1)} copy-done((bf16[1,1,2048,2048]{3,2,1,0:T(8,128)(2,1)S(1)}, bf16[1,1,2048,2048]{3,2,1,0:T(8,128)(2,1)}, u32[]{:S(2)}) %copy-start.1) | copy-done | bytes 8388632
  33.7 3.7 %shard_map.123 = (f32[64,2048]{1,0:T(8,128)S(1)}, f32[64,2048]{1,0:T(8,128)S(1)}, f32[64,512]{1,0:T(8,128)}, f32[64,512]{1,0:T(8,128)}, f32[64,512]{1,0:T(8,128)...) custom-call(s32[4]{0:T(128)S(1)} %pad_add_fusion.order, ...), custom_call_target="tpu_custom_call" | custom-call | flops 536870912 | bytes 3135488 | tf_op jit(solution)/shard_map/pallas_call | solution.py:322
  37.5 22.5 %all_to_all.24 = f32[64,16,128]{2,1,0:T(8,128)S(1)} all-to-all(f32[64,16,128]{2,1,0:T(8,128)S(1)} %broadcast_in_dim.12), channel_id=1, replica_groups={{0,1,2,3,4,5,6,7,8,9,10,11,12,13,14,15,32,33,34,35,36,37,38,39,40,41,42..., dimensions={0} | all-to-all | bytes 1048576 | tf_op jit(solution)/shard_map/all_to_all | solution.py:429
  59.9 2.2 %shard_map.124 = (f32[456,128]{1,0:T(8,128)S(1)}, bf16[2,896,1024]{2,1,0:T(8,128)(2,1)S(1)}) custom-call(f32[1024,128]{1,0:T(8,128)S(1)} %bitcast.62), custom_call_target="tpu_custom_call" | custom-call | flops 8000000000 | bytes 131072 | tf_op jit(solution)/shard_map/pallas_call | solution.py:322
  62.1 1.8 copy-done.17
  63.9 2.9 %collective-permute-start.4 = (f32[456,128]{1,0:T(8,128)S(1)}, f32[456,128]{1,0:T(8,128)S(1)}, u32[]{:S(2)}, u32[]{:S(2)}) collective-permute-start(f32[456,128]{1,0:T(8,128)S(1)} %get-tuple-element.84.refs_0_), channel_id=1, source_target_pairs={{0,16},{16,0},{32,48},{48,32},{64,80},{80,64},{96,112},{112,96},{1... | collective-permute-start | bytes 700424 | tf_op jit(solution)/shard_map/ppermute | solution.py:25
  70.1 2.1 %copy-done.9 = f32[896,896]{1,0:T(8,128)S(1)} copy-done((f32[896,896]{1,0:T(8,128)S(1)}, f32[896,896]{1,0:T(8,128)}, u32[]{:S(2)}) %copy-start.9) | copy-done | bytes 3211288
  72.2 1.7 copy-done.11
  78.0 3.8 %shard_map.126 = (f32[64,2048]{1,0:T(8,128)S(1)}, f32[64,2048]{1,0:T(8,128)S(1)}, f32[64,512]{1,0:T(8,128)S(1)}, f32[64,512]{1,0:T(8,128)S(1)}, f32[64,512]{1,0:...) custom-call(s32[4]{0:T(128)S(1)} %pad_add_fusion.order, f32[160,128]{1,0:T(8,128)S(1)} %get-tuple-element.86.refs_0_, ...), custom_call_target="tpu_custom_call" | custom-call | flops 536870912 | bytes 2973696 | tf_op jit(solution)/shard_map/pallas_call | solution.py:322
  84.0 3.7 %collective-permute-start.12 = (f32[64,512]{1,0:T(8,128)S(1)}, f32[64,512]{1,0:T(8,128)S(1)}, u32[]{:S(2)}, u32[]{:S(2)}) collective-permute-start(f32[64,512]{1,0:T(8,128)S(1)} %get-tuple-element.96), channel_id=1, source_target_pairs={{1,2},{2,1},{3,4},{4,3},{5,6},{6,5},{7,8},{8,7},{9,10},{10,9},{11,... | collective-permute-start | bytes 393224 | tf_op jit(solution)/shard_map/ppermute | solution.py:25
  88.2 3.0 %collective-permute-done.12.refs_3_ = f32[64,512]{1,0:T(8,128)S(1)} collective-permute-done((f32[64,512]{1,0:T(8,128)S(1)}, f32[64,512]{1,0:T(8,128)S(1)}, u32[]{:S(2)}, u32[]{:S(2)}) %collective-permute-start.12) | collective-permute-done | bytes 131104 | tf_op jit(solution)/shard_map/ppermute | solution.py:25
  91.2 3.2 %shard_map.127 = (f32[64,2048]{1,0:T(8,128)S(1)}, f32[64,2048]{1,0:T(8,128)S(1)}, f32[64,512]{1,0:T(8,128)S(1)}, f32[64,512]{1,0:T(8,128)S(1)}, f32[64,512]{1,0:...) custom-call(s32[4]{0:T(128)S(1)} %pad_add_fusion.order, f32[64,512]{1,0:T(8,128)S(1)} %collective-permute-done.9.refs_0_, ...), custom_call_target="tpu_custom_call" | custom-call | flops 536870912 | bytes 2926592 | tf_op jit(solution)/shard_map/pallas_call | solution.py:322
  94.4 21.0 %all_to_all.25 = f32[64,16,128]{2,1,0:T(8,128)S(1)} all-to-all(f32[64,16,128]{2,1,0:T(8,128)S(1)} %broadcast_in_dim.13), channel_id=1, replica_groups={{0,1,2,3,4,5,6,7,8,9,10,11,12,13,14,15,32,33,34,35,36,37,38,39,40,41,42..., dimensions={0} | all-to-all | bytes 1048576 | tf_op jit(solution)/shard_map/all_to_all | solution.py:429
  116.7 2.4 %collective-permute-start.13 = (f32[456,128]{1,0:T(8,128)S(1)}, f32[456,128]{1,0:T(8,128)S(1)}, u32[]{:S(2)}, u32[]{:S(2)}) collective-permute-start(f32[456,128]{1,0:T(8,128)S(1)} %shard_map.128.refs_0_), channel_id=1, source_target_pairs={{0,16},{16,0},{32,48},{48,32},{64,80},{80,64},{96,112},{112,96},{1... | collective-permute-start | bytes 700424 | tf_op jit(solution)/shard_map/ppermute | solution.py:25
  123.9 3.0 %collective-permute-done.17.refs_4_ = f32[64,512]{1,0:T(8,128)S(1)} collective-permute-done((f32[64,512]{1,0:T(8,128)S(1)}, f32[64,512]{1,0:T(8,128)S(1)}, u32[]{:S(2)}, u32[]{:S(2)}) %collective-permute-start.17) | collective-permute-done | bytes 131104 | tf_op jit(solution)/shard_map/ppermute | solution.py:25
  126.9 3.1 %shard_map.130 = (f32[64,2048]{1,0:T(8,128)S(1)}, f32[64,2048]{1,0:T(8,128)S(1)}, f32[64,512]{1,0:T(8,128)S(1)}, f32[64,512]{1,0:T(8,128)S(1)}, f32[64,512]{1,0:...) custom-call(s32[4]{0:T(128)S(1)} %pad_add_fusion.order, ...), custom_call_target="tpu_custom_call" | custom-call | flops 536870912 | bytes 3375104 | tf_op jit(solution)/shard_map/pallas_call | solution.py:322
  129.9 2.2 %collective-permute-start.18 = (f32[64,512]{1,0:T(8,128)S(1)}, f32[64,512]{1,0:T(8,128)S(1)}, u32[]{:S(2)}, u32[]{:S(2)}) collective-permute-start(f32[64,512]{1,0:T(8,128)S(1)} %get-tuple-element.113), channel_id=1, source_target_pairs={{0,16},{16,0},{32,48},{48,32},{64,80},{80,64},{96,112},{112,96},{1... | collective-permute-start | bytes 393224 | tf_op jit(solution)/shard_map/ppermute | solution.py:25
  134.1 2.7 %collective-permute-done.19.refs_1_ = f32[64,512]{1,0:T(8,128)S(1)} collective-permute-done((f32[64,512]{1,0:T(8,128)S(1)}, f32[64,512]{1,0:T(8,128)S(1)}, u32[]{:S(2)}, u32[]{:S(2)}) %collective-permute-start.19) | collective-permute-done | bytes 131104 | tf_op jit(solution)/shard_map/ppermute | solution.py:25
  137.8 3.3 %collective-permute-done.21.refs_3_ = f32[64,512]{1,0:T(8,128)S(1)} collective-permute-done((f32[64,512]{1,0:T(8,128)S(1)}, f32[64,512]{1,0:T(8,128)S(1)}, u32[]{:S(2)}, u32[]{:S(2)}) %collective-permute-start.21) | collective-permute-done | bytes 131104 | tf_op jit(solution)/shard_map/ppermute | solution.py:25
  141.1 3.1 %shard_map.131 = (f32[64,2048]{1,0:T(8,128)S(1)}, f32[64,2048]{1,0:T(8,128)S(1)}, f32[64,512]{1,0:T(8,128)S(1)}, f32[64,512]{1,0:T(8,128)S(1)}, f32[64,512]{1,0:...) custom-call(s32[4]{0:T(128)S(1)} %pad_add_fusion.order, f32[64,512]{1,0:T(8,128)S(1)} %collective-permute-done.18.refs_0_, ...), custom_call_target="tpu_custom_call" | custom-call | flops 536870912 | bytes 3057664 | tf_op jit(solution)/shard_map/pallas_call | solution.py:322
  144.2 17.6 %all_to_all.26 = f32[64,16,128]{2,1,0:T(8,128)S(1)} all-to-all(f32[64,16,128]{2,1,0:T(8,128)S(1)} %broadcast_in_dim.14), channel_id=1, replica_groups={{0,1,2,3,4,5,6,7,8,9,10,11,12,13,14,15,32,33,34,35,36,37,38,39,40,41,42..., dimensions={0} | all-to-all | bytes 1048576 | tf_op jit(solution)/shard_map/all_to_all | solution.py:429
  163.1 2.4 %collective-permute-start.22 = (f32[456,128]{1,0:T(8,128)S(1)}, f32[456,128]{1,0:T(8,128)S(1)}, u32[]{:S(2)}, u32[]{:S(2)}) collective-permute-start(f32[456,128]{1,0:T(8,128)S(1)} %shard_map.132.refs_0_), channel_id=1, source_target_pairs={{0,16},{16,0},{32,48},{48,32},{64,80},{80,64},{96,112},{112,96},{1... | collective-permute-start | bytes 700424 | tf_op jit(solution)/shard_map/ppermute | solution.py:25
  167.6 1.7 shard_map.133
  170.3 3.0 %collective-permute-done.26.refs_4_ = f32[64,512]{1,0:T(8,128)S(1)} collective-permute-done((f32[64,512]{1,0:T(8,128)S(1)}, f32[64,512]{1,0:T(8,128)S(1)}, u32[]{:S(2)}, u32[]{:S(2)}) %collective-permute-start.26) | collective-permute-done | bytes 131104 | tf_op jit(solution)/shard_map/ppermute | solution.py:25
  173.3 3.5 %shard_map.134 = (f32[64,2048]{1,0:T(8,128)}, f32[64,2048]{1,0:T(8,128)S(1)}, f32[64,512]{1,0:T(8,128)S(1)}, f32[64,512]{1,0:T(8,128)S(1)}, f32[64,512]{1,0:T(8,...) custom-call(s32[4]{0:T(128)S(1)} %pad_add_fusion.order, f32[160,128]{1,0:T(8,128)S(1)} %get-tuple-element.122.refs_0_, ...), custom_call_target="tpu_custom_call" | custom-call | flops 536870912 | bytes 3645440 | tf_op jit(solution)/shard_map/pallas_call | solution.py:322
  176.8 2.2 %collective-permute-start.27 = (f32[64,512]{1,0:T(8,128)S(1)}, f32[64,512]{1,0:T(8,128)S(1)}, u32[]{:S(2)}, u32[]{:S(2)}) collective-permute-start(f32[64,512]{1,0:T(8,128)S(1)} %get-tuple-element.136), channel_id=1, source_target_pairs={{0,16},{16,0},{32,48},{48,32},{64,80},{80,64},{96,112},{112,96},{1... | collective-permute-start | bytes 393224 | tf_op jit(solution)/shard_map/ppermute | solution.py:25
  180.8 2.8 %collective-permute-done.28.refs_1_ = f32[64,512]{1,0:T(8,128)S(1)} collective-permute-done((f32[64,512]{1,0:T(8,128)S(1)}, f32[64,512]{1,0:T(8,128)S(1)}, u32[]{:S(2)}, u32[]{:S(2)}) %collective-permute-start.28) | collective-permute-done | bytes 131104 | tf_op jit(solution)/shard_map/ppermute | solution.py:25
  184.4 3.3 %collective-permute-done.30.refs_3_ = f32[64,512]{1,0:T(8,128)S(1)} collective-permute-done((f32[64,512]{1,0:T(8,128)S(1)}, f32[64,512]{1,0:T(8,128)S(1)}, u32[]{:S(2)}, u32[]{:S(2)}) %collective-permute-start.30) | collective-permute-done | bytes 131104 | tf_op jit(solution)/shard_map/ppermute | solution.py:25
  187.8 1.9 shard_map.135
  (110 shorter events, 38.8 us)
Async XLA Ops:
  7.2 62.9 %all-gather.2.cloned.1.call-start = ((), (), s32[]{:S(2)}) async-start(), calls=%async_computation.3 | async-start | bytes 3411968 | tf_op jit(solution)/shard_map/all_gather | solution.py:365
  12.8 18.3 %collective-permute-start = (f32[104,512]{1,0:T(8,128)S(1)}, f32[104,512]{1,0:T(8,128)S(1)}, u32[]{:S(2)}, u32[]{:S(2)}) collective-permute-start(f32[104,512]{1,0:T(8,128)S(1)} %get-tuple-element.78), channel_id=1, source_target_pairs={{0,16},{16,0},{32,48},{48,32},{64,80},{80,64},{96,112},{112,96},{1... | collective-permute-start | bytes 638984 | tf_op jit(solution)/shard_map/ppermute | solution.py:25
  14.3 16.8 %collective-permute-start.1 = (f32[104,512]{1,0:T(8,128)S(1)}, f32[104,512]{1,0:T(8,128)S(1)}, u32[]{:S(2)}, u32[]{:S(2)}) collective-permute-start(f32[104,512]{1,0:T(8,128)S(1)} %get-tuple-element.79), channel_id=1, source_target_pairs={{16,32},{32,16},{48,64},{64,48},{80,96},{96,80},{112,0},{0,112},{1... | collective-permute-start | bytes 638984 | tf_op jit(solution)/shard_map/ppermute | solution.py:25
  15.6 15.4 %collective-permute-start.2 = (f32[104,512]{1,0:T(8,128)S(1)}, f32[104,512]{1,0:T(8,128)S(1)}, u32[]{:S(2)}, u32[]{:S(2)}) collective-permute-start(f32[104,512]{1,0:T(8,128)S(1)} %get-tuple-element.80), channel_id=1, source_target_pairs={{0,1},{1,0},{2,3},{3,2},{4,5},{5,4},{6,7},{7,6},{8,9},{9,8},{10,11... | collective-permute-start | bytes 638984 | tf_op jit(solution)/shard_map/ppermute | solution.py:25
  17.3 13.8 %collective-permute-start.3 = (f32[104,512]{1,0:T(8,128)S(1)}, f32[104,512]{1,0:T(8,128)S(1)}, u32[]{:S(2)}, u32[]{:S(2)}) collective-permute-start(f32[104,512]{1,0:T(8,128)S(1)} %get-tuple-element.81), channel_id=1, source_target_pairs={{1,2},{2,1},{3,4},{4,3},{5,6},{6,5},{7,8},{8,7},{9,10},{10,9},{11,... | collective-permute-start | bytes 638984 | tf_op jit(solution)/shard_map/ppermute | solution.py:25
  63.9 5.5 %collective-permute-start.4 = (f32[456,128]{1,0:T(8,128)S(1)}, f32[456,128]{1,0:T(8,128)S(1)}, u32[]{:S(2)}, u32[]{:S(2)}) collective-permute-start(f32[456,128]{1,0:T(8,128)S(1)} %get-tuple-element.84.refs_0_), channel_id=1, source_target_pairs={{0,16},{16,0},{32,48},{48,32},{64,80},{80,64},{96,112},{112,96},{1... | collective-permute-start | bytes 700424 | tf_op jit(solution)/shard_map/ppermute | solution.py:25
  67.5 9.9 %collective-permute-start.5 = (f32[64,512]{1,0:T(8,128)}, f32[64,512]{1,0:T(8,128)}, u32[]{:S(2)}, u32[]{:S(2)}) collective-permute-start(f32[64,512]{1,0:T(8,128)} %get-tuple-element.87), channel_id=1, source_target_pairs={{0,16},{16,0},{32,48},{48,32},{64,80},{80,64},{96,112},{112,96},{1... | collective-permute-start | bytes 393224 | tf_op jit(solution)/shard_map/ppermute | solution.py:25
  67.5 9.9 %collective-permute-start.6 = (f32[64,512]{1,0:T(8,128)}, f32[64,512]{1,0:T(8,128)}, u32[]{:S(2)}, u32[]{:S(2)}) collective-permute-start(f32[64,512]{1,0:T(8,128)} %get-tuple-element.88), channel_id=1, source_target_pairs={{16,32},{32,16},{48,64},{64,48},{80,96},{96,80},{112,0},{0,112},{1... | collective-permute-start | bytes 393224 | tf_op jit(solution)/shard_map/ppermute | solution.py:25
  67.5 9.9 %collective-permute-start.7 = (f32[64,512]{1,0:T(8,128)}, f32[64,512]{1,0:T(8,128)}, u32[]{:S(2)}, u32[]{:S(2)}) collective-permute-start(f32[64,512]{1,0:T(8,128)} %get-tuple-element.89), channel_id=1, source_target_pairs={{0,1},{1,0},{2,3},{3,2},{4,5},{5,4},{6,7},{7,6},{8,9},{9,8},{10,11... | collective-permute-start | bytes 393224 | tf_op jit(solution)/shard_map/ppermute | solution.py:25
  68.0 9.4 %collective-permute-start.8 = (f32[64,512]{1,0:T(8,128)}, f32[64,512]{1,0:T(8,128)}, u32[]{:S(2)}, u32[]{:S(2)}) collective-permute-start(f32[64,512]{1,0:T(8,128)} %get-tuple-element.90), channel_id=1, source_target_pairs={{1,2},{2,1},{3,4},{4,3},{5,6},{6,5},{7,8},{8,7},{9,10},{10,9},{11,... | collective-permute-start | bytes 393224 | tf_op jit(solution)/shard_map/ppermute | solution.py:25
  81.8 5.9 %collective-permute-start.9 = (f32[64,512]{1,0:T(8,128)S(1)}, f32[64,512]{1,0:T(8,128)S(1)}, u32[]{:S(2)}, u32[]{:S(2)}) collective-permute-start(f32[64,512]{1,0:T(8,128)S(1)} %get-tuple-element.93), channel_id=1, source_target_pairs={{0,16},{16,0},{32,48},{48,32},{64,80},{80,64},{96,112},{112,96},{1... | collective-permute-start | bytes 393224 | tf_op jit(solution)/shard_map/ppermute | solution.py:25
  83.1 4.7 %collective-permute-start.10 = (f32[64,512]{1,0:T(8,128)S(1)}, f32[64,512]{1,0:T(8,128)S(1)}, u32[]{:S(2)}, u32[]{:S(2)}) collective-permute-start(f32[64,512]{1,0:T(8,128)S(1)} %get-tuple-element.94), channel_id=1, source_target_pairs={{16,32},{32,16},{48,64},{64,48},{80,96},{96,80},{112,0},{0,112},{1... | collective-permute-start | bytes 393224 | tf_op jit(solution)/shard_map/ppermute | solution.py:25
  84.0 4.1 %collective-permute-start.11 = (f32[64,512]{1,0:T(8,128)S(1)}, f32[64,512]{1,0:T(8,128)S(1)}, u32[]{:S(2)}, u32[]{:S(2)}) collective-permute-start(f32[64,512]{1,0:T(8,128)S(1)} %get-tuple-element.95), channel_id=1, source_target_pairs={{0,1},{1,0},{2,3},{3,2},{4,5},{5,4},{6,7},{7,6},{8,9},{9,8},{10,11... | collective-permute-start | bytes 393224 | tf_op jit(solution)/shard_map/ppermute | solution.py:25
  84.0 7.1 %collective-permute-start.12 = (f32[64,512]{1,0:T(8,128)S(1)}, f32[64,512]{1,0:T(8,128)S(1)}, u32[]{:S(2)}, u32[]{:S(2)}) collective-permute-start(f32[64,512]{1,0:T(8,128)S(1)} %get-tuple-element.96), channel_id=1, source_target_pairs={{1,2},{2,1},{3,4},{4,3},{5,6},{6,5},{7,8},{8,7},{9,10},{10,9},{11,... | collective-permute-start | bytes 393224 | tf_op jit(solution)/shard_map/ppermute | solution.py:25
  116.7 4.5 %collective-permute-start.13 = (f32[456,128]{1,0:T(8,128)S(1)}, f32[456,128]{1,0:T(8,128)S(1)}, u32[]{:S(2)}, u32[]{:S(2)}) collective-permute-start(f32[456,128]{1,0:T(8,128)S(1)} %shard_map.128.refs_0_), channel_id=1, source_target_pairs={{0,16},{16,0},{32,48},{48,32},{64,80},{80,64},{96,112},{112,96},{1... | collective-permute-start | bytes 700424 | tf_op jit(solution)/shard_map/ppermute | solution.py:25
  119.1 3.7 %collective-permute-start.14 = (f32[64,512]{1,0:T(8,128)S(1)}, f32[64,512]{1,0:T(8,128)S(1)}, u32[]{:S(2)}, u32[]{:S(2)}) collective-permute-start(f32[64,512]{1,0:T(8,128)S(1)} %get-tuple-element.104), channel_id=1, source_target_pairs={{0,16},{16,0},{32,48},{48,32},{64,80},{80,64},{96,112},{112,96},{1... | collective-permute-start | bytes 393224 | tf_op jit(solution)/shard_map/ppermute | solution.py:25
  119.2 4.7 %collective-permute-start.15 = (f32[64,512]{1,0:T(8,128)S(1)}, f32[64,512]{1,0:T(8,128)S(1)}, u32[]{:S(2)}, u32[]{:S(2)}) collective-permute-start(f32[64,512]{1,0:T(8,128)S(1)} %get-tuple-element.105), channel_id=1, source_target_pairs={{16,32},{32,16},{48,64},{64,48},{80,96},{96,80},{112,0},{0,112},{1... | collective-permute-start | bytes 393224 | tf_op jit(solution)/shard_map/ppermute | solution.py:25
  119.4 4.5 %collective-permute-start.16 = (f32[64,512]{1,0:T(8,128)S(1)}, f32[64,512]{1,0:T(8,128)S(1)}, u32[]{:S(2)}, u32[]{:S(2)}) collective-permute-start(f32[64,512]{1,0:T(8,128)S(1)} %get-tuple-element.106), channel_id=1, source_target_pairs={{0,1},{1,0},{2,3},{3,2},{4,5},{5,4},{6,7},{7,6},{8,9},{9,8},{10,11... | collective-permute-start | bytes 393224 | tf_op jit(solution)/shard_map/ppermute | solution.py:25
  119.7 7.1 %collective-permute-start.17 = (f32[64,512]{1,0:T(8,128)S(1)}, f32[64,512]{1,0:T(8,128)S(1)}, u32[]{:S(2)}, u32[]{:S(2)}) collective-permute-start(f32[64,512]{1,0:T(8,128)S(1)} %get-tuple-element.107), channel_id=1, source_target_pairs={{1,2},{2,1},{3,4},{4,3},{5,6},{6,5},{7,8},{8,7},{9,10},{10,9},{11,... | collective-permute-start | bytes 393224 | tf_op jit(solution)/shard_map/ppermute | solution.py:25
  129.9 4.2 %collective-permute-start.18 = (f32[64,512]{1,0:T(8,128)S(1)}, f32[64,512]{1,0:T(8,128)S(1)}, u32[]{:S(2)}, u32[]{:S(2)}) collective-permute-start(f32[64,512]{1,0:T(8,128)S(1)} %get-tuple-element.113), channel_id=1, source_target_pairs={{0,16},{16,0},{32,48},{48,32},{64,80},{80,64},{96,112},{112,96},{1... | collective-permute-start | bytes 393224 | tf_op jit(solution)/shard_map/ppermute | solution.py:25
  132.2 4.7 %collective-permute-start.19 = (f32[64,512]{1,0:T(8,128)S(1)}, f32[64,512]{1,0:T(8,128)S(1)}, u32[]{:S(2)}, u32[]{:S(2)}) collective-permute-start(f32[64,512]{1,0:T(8,128)S(1)} %get-tuple-element.114), channel_id=1, source_target_pairs={{16,32},{32,16},{48,64},{64,48},{80,96},{96,80},{112,0},{0,112},{1... | collective-permute-start | bytes 393224 | tf_op jit(solution)/shard_map/ppermute | solution.py:25
  133.1 4.7 %collective-permute-start.20 = (f32[64,512]{1,0:T(8,128)S(1)}, f32[64,512]{1,0:T(8,128)S(1)}, u32[]{:S(2)}, u32[]{:S(2)}) collective-permute-start(f32[64,512]{1,0:T(8,128)S(1)} %get-tuple-element.115), channel_id=1, source_target_pairs={{0,1},{1,0},{2,3},{3,2},{4,5},{5,4},{6,7},{7,6},{8,9},{9,8},{10,11... | collective-permute-start | bytes 393224 | tf_op jit(solution)/shard_map/ppermute | solution.py:25
  133.1 8.0 %collective-permute-start.21 = (f32[64,512]{1,0:T(8,128)S(1)}, f32[64,512]{1,0:T(8,128)S(1)}, u32[]{:S(2)}, u32[]{:S(2)}) collective-permute-start(f32[64,512]{1,0:T(8,128)S(1)} %get-tuple-element.116), channel_id=1, source_target_pairs={{1,2},{2,1},{3,4},{4,3},{5,6},{6,5},{7,8},{8,7},{9,10},{10,9},{11,... | collective-permute-start | bytes 393224 | tf_op jit(solution)/shard_map/ppermute | solution.py:25
  163.1 4.5 %collective-permute-start.22 = (f32[456,128]{1,0:T(8,128)S(1)}, f32[456,128]{1,0:T(8,128)S(1)}, u32[]{:S(2)}, u32[]{:S(2)}) collective-permute-start(f32[456,128]{1,0:T(8,128)S(1)} %shard_map.132.refs_0_), channel_id=1, source_target_pairs={{0,16},{16,0},{32,48},{48,32},{64,80},{80,64},{96,112},{112,96},{1... | collective-permute-start | bytes 700424 | tf_op jit(solution)/shard_map/ppermute | solution.py:25
  165.5 3.8 %collective-permute-start.23 = (f32[64,512]{1,0:T(8,128)S(1)}, f32[64,512]{1,0:T(8,128)S(1)}, u32[]{:S(2)}, u32[]{:S(2)}) collective-permute-start(f32[64,512]{1,0:T(8,128)S(1)} %get-tuple-element.123), channel_id=1, source_target_pairs={{0,16},{16,0},{32,48},{48,32},{64,80},{80,64},{96,112},{112,96},{1... | collective-permute-start | bytes 393224 | tf_op jit(solution)/shard_map/ppermute | solution.py:25
  165.6 4.7 %collective-permute-start.24 = (f32[64,512]{1,0:T(8,128)S(1)}, f32[64,512]{1,0:T(8,128)S(1)}, u32[]{:S(2)}, u32[]{:S(2)}) collective-permute-start(f32[64,512]{1,0:T(8,128)S(1)} %get-tuple-element.124), channel_id=1, source_target_pairs={{16,32},{32,16},{48,64},{64,48},{80,96},{96,80},{112,0},{0,112},{1... | collective-permute-start | bytes 393224 | tf_op jit(solution)/shard_map/ppermute | solution.py:25
  165.7 4.5 %collective-permute-start.25 = (f32[64,512]{1,0:T(8,128)S(1)}, f32[64,512]{1,0:T(8,128)S(1)}, u32[]{:S(2)}, u32[]{:S(2)}) collective-permute-start(f32[64,512]{1,0:T(8,128)S(1)} %get-tuple-element.125), channel_id=1, source_target_pairs={{0,1},{1,0},{2,3},{3,2},{4,5},{5,4},{6,7},{7,6},{8,9},{9,8},{10,11... | collective-permute-start | bytes 393224 | tf_op jit(solution)/shard_map/ppermute | solution.py:25
  166.1 7.1 %collective-permute-start.26 = (f32[64,512]{1,0:T(8,128)S(1)}, f32[64,512]{1,0:T(8,128)S(1)}, u32[]{:S(2)}, u32[]{:S(2)}) collective-permute-start(f32[64,512]{1,0:T(8,128)S(1)} %get-tuple-element.126), channel_id=1, source_target_pairs={{1,2},{2,1},{3,4},{4,3},{5,6},{6,5},{7,8},{8,7},{9,10},{10,9},{11,... | collective-permute-start | bytes 393224 | tf_op jit(solution)/shard_map/ppermute | solution.py:25
  176.8 4.1 %collective-permute-start.27 = (f32[64,512]{1,0:T(8,128)S(1)}, f32[64,512]{1,0:T(8,128)S(1)}, u32[]{:S(2)}, u32[]{:S(2)}) collective-permute-start(f32[64,512]{1,0:T(8,128)S(1)} %get-tuple-element.136), channel_id=1, source_target_pairs={{0,16},{16,0},{32,48},{48,32},{64,80},{80,64},{96,112},{112,96},{1... | collective-permute-start | bytes 393224 | tf_op jit(solution)/shard_map/ppermute | solution.py:25
  179.0 4.7 %collective-permute-start.28 = (f32[64,512]{1,0:T(8,128)S(1)}, f32[64,512]{1,0:T(8,128)S(1)}, u32[]{:S(2)}, u32[]{:S(2)}) collective-permute-start(f32[64,512]{1,0:T(8,128)S(1)} %get-tuple-element.137), channel_id=1, source_target_pairs={{16,32},{32,16},{48,64},{64,48},{80,96},{96,80},{112,0},{0,112},{1... | collective-permute-start | bytes 393224 | tf_op jit(solution)/shard_map/ppermute | solution.py:25
  179.8 4.7 %collective-permute-start.29 = (f32[64,512]{1,0:T(8,128)S(1)}, f32[64,512]{1,0:T(8,128)S(1)}, u32[]{:S(2)}, u32[]{:S(2)}) collective-permute-start(f32[64,512]{1,0:T(8,128)S(1)} %get-tuple-element.138), channel_id=1, source_target_pairs={{0,1},{1,0},{2,3},{3,2},{4,5},{5,4},{6,7},{7,6},{8,9},{9,8},{10,11... | collective-permute-start | bytes 393224 | tf_op jit(solution)/shard_map/ppermute | solution.py:25
  179.8 8.0 %collective-permute-start.30 = (f32[64,512]{1,0:T(8,128)S(1)}, f32[64,512]{1,0:T(8,128)S(1)}, u32[]{:S(2)}, u32[]{:S(2)}) collective-permute-start(f32[64,512]{1,0:T(8,128)S(1)} %get-tuple-element.139), channel_id=1, source_target_pairs={{1,2},{2,1},{3,4},{4,3},{5,6},{6,5},{7,8},{8,7},{9,10},{10,9},{11,... | collective-permute-start | bytes 393224 | tf_op jit(solution)/shard_map/ppermute | solution.py:25
  (23 other events, 131.9 us)
Sparse Core Ops, SparseCore 0:
  10.2 56.1 all-gather.1

commit v3 on v2

--- a/solution.py
+++ b/solution.py
@@ -55,9 +55,9 @@
 
 
 def picked(came, picker, link, rows):
-    stacked = jnp.concatenate(parts_of(came[link][0:rows, :], 3), axis=0)
+    stacked = jnp.concatenate(parts_of(came[link][0:rows, :], 2), axis=0)
     got = dot(stacked, picker[link])
-    return got[:rows] + got[rows : 2 * rows] + got[2 * rows :]
+    return got[:rows] + got[rows:]
 
 
 def column(row, rows):

time: 197 us -> 195 us (0.990)
  no operation moved by 1% of the time
where the time goes in v3:
time: 195 us
  blocking collectives  60 us (31%)
  starting transfers between devices  37.7 us (19%)
  Pallas kernels  32.1 us (16%)
  waiting for transfers between devices  25.5 us (13%)
  local copies, waits for them, and re-layouts  23.9 us (12%)
  between operations  14.3 us (7%)
    all_to_all x3, blocking collectives, gather(): lax.all_to_all(many, BOTH, split_axis=0, concat_axis=0, tiled=True, axis_...  60 us
    ppermute x31, starting transfers between devices, swap(): return lax.ppermute(block, axis, route)  37.6 us
    pallas_call x15, Pallas kernels, call(): pl.pallas_call(kernel, out_shape=[s if hasattr(s, 'dtype') else jax.Shape...  32.1 us
    ppermute x31, waiting for transfers between devices, swap(): return lax.ppermute(block, axis, route)  25.5 us
    unnamed x47, local copies, waits for them, and re-layouts  21.6 us
  transfers between devices with their start and end apart: 32, of which 12 were waited for; matrix products, arithmetic and copies ran while one was open for 1% of the time, Pallas kernels for 6%

profile of v3, /device:TPU:1, one launch (start us, length us, event | category | flops | bytes accessed | tf_op | source)
XLA Modules:
  0.0 195.0 jit_solution(7297261788614581543)
XLA Ops:
  17.3 4.4 %collective-permute-start.3 = (f32[104,512]{1,0:T(8,128)S(1)}, f32[104,512]{1,0:T(8,128)S(1)}, u32[]{:S(2)}, u32[]{:S(2)}) collective-permute-start(f32[104,512]{1,0:T(8,128)S(1)} %get-tuple-element.81), channel_id=1, source_target_pairs={{1,2},{2,1},{3,4},{4,3},{5,6},{6,5},{7,8},{8,7},{9,10},{10,9},{11,... | collective-permute-start | bytes 638984 | tf_op jit(solution)/shard_map/ppermute | solution.py:25
  22.5 3.5 %copy-done = bf16[1,1,2048,2048]{3,2,1,0:T(8,128)(2,1)S(1)} copy-done((bf16[1,1,2048,2048]{3,2,1,0:T(8,128)(2,1)S(1)}, bf16[1,1,2048,2048]{3,2,1,0:T(8,128)(2,1)}, u32[]{:S(2)}) %copy-start) | copy-done | bytes 8388632
  26.0 3.4 %copy-done.2 = bf16[1,1,2048,2048]{3,2,1,0:T(8,128)(2,1)S(1)} copy-done((bf16[1,1,2048,2048]{3,2,1,0:T(8,128)(2,1)S(1)}, bf16[1,1,2048,2048]{3,2,1,0:T(8,128)(2,1)}, u32[]{:S(2)}) %copy-start.2) | copy-done | bytes 8388632
  31.1 2.4 %copy-done.1 = bf16[1,1,2048,2048]{3,2,1,0:T(8,128)(2,1)S(1)} copy-done((bf16[1,1,2048,2048]{3,2,1,0:T(8,128)(2,1)S(1)}, bf16[1,1,2048,2048]{3,2,1,0:T(8,128)(2,1)}, u32[]{:S(2)}) %copy-start.1) | copy-done | bytes 8388632
  33.7 3.2 %shard_map.123 = (f32[64,2048]{1,0:T(8,128)S(1)}, f32[64,2048]{1,0:T(8,128)S(1)}, f32[64,512]{1,0:T(8,128)}, f32[64,512]{1,0:T(8,128)}, f32[64,512]{1,0:T(8,128)...) custom-call(s32[4]{0:T(128)S(1)} %pad_add_fusion.order, ...), custom_call_target="tpu_custom_call" | custom-call | flops 536870912 | bytes 3135488 | tf_op jit(solution)/shard_map/pallas_call | solution.py:322
  37.0 21.4 %all_to_all.24 = f32[64,16,128]{2,1,0:T(8,128)S(1)} all-to-all(f32[64,16,128]{2,1,0:T(8,128)S(1)} %broadcast_in_dim.12), channel_id=1, replica_groups={{0,1,2,3,4,5,6,7,8,9,10,11,12,13,14,15,32,33,34,35,36,37,38,39,40,41,42..., dimensions={0} | all-to-all | bytes 1048576 | tf_op jit(solution)/shard_map/all_to_all | solution.py:429
  58.4 2.2 %shard_map.124 = (f32[456,128]{1,0:T(8,128)S(1)}, bf16[2,896,1024]{2,1,0:T(8,128)(2,1)S(1)}) custom-call(f32[1024,128]{1,0:T(8,128)S(1)} %bitcast.62), custom_call_target="tpu_custom_call" | custom-call | flops 8000000000 | bytes 131072 | tf_op jit(solution)/shard_map/pallas_call | solution.py:322
  60.6 1.8 copy-done.17
  62.4 3.7 %collective-permute-start.4 = (f32[456,128]{1,0:T(8,128)S(1)}, f32[456,128]{1,0:T(8,128)S(1)}, u32[]{:S(2)}, u32[]{:S(2)}) collective-permute-start(f32[456,128]{1,0:T(8,128)S(1)} %get-tuple-element.84.refs_0_), channel_id=1, source_target_pairs={{0,16},{16,0},{32,48},{48,32},{64,80},{80,64},{96,112},{112,96},{1... | collective-permute-start | bytes 700424 | tf_op jit(solution)/shard_map/ppermute | solution.py:25
  69.4 2.1 %copy-done.9 = f32[896,896]{1,0:T(8,128)S(1)} copy-done((f32[896,896]{1,0:T(8,128)S(1)}, f32[896,896]{1,0:T(8,128)}, u32[]{:S(2)}) %copy-start.9) | copy-done | bytes 3211288
  71.5 1.7 copy-done.11
  77.3 3.7 %shard_map.126 = (f32[64,2048]{1,0:T(8,128)S(1)}, f32[64,2048]{1,0:T(8,128)S(1)}, f32[64,512]{1,0:T(8,128)S(1)}, f32[64,512]{1,0:T(8,128)S(1)}, f32[64,512]{1,0:...) custom-call(s32[4]{0:T(128)S(1)} %pad_add_fusion.order, f32[160,128]{1,0:T(8,128)S(1)} %get-tuple-element.86.refs_0_, ...), custom_call_target="tpu_custom_call" | custom-call | flops 536870912 | bytes 2973696 | tf_op jit(solution)/shard_map/pallas_call | solution.py:322
  83.2 3.6 %collective-permute-start.12 = (f32[64,512]{1,0:T(8,128)S(1)}, f32[64,512]{1,0:T(8,128)S(1)}, u32[]{:S(2)}, u32[]{:S(2)}) collective-permute-start(f32[64,512]{1,0:T(8,128)S(1)} %get-tuple-element.96), channel_id=1, source_target_pairs={{1,2},{2,1},{3,4},{4,3},{5,6},{6,5},{7,8},{8,7},{9,10},{10,9},{11,... | collective-permute-start | bytes 393224 | tf_op jit(solution)/shard_map/ppermute | solution.py:25
  87.3 3.0 %collective-permute-done.12.refs_3_ = f32[64,512]{1,0:T(8,128)S(1)} collective-permute-done((f32[64,512]{1,0:T(8,128)S(1)}, f32[64,512]{1,0:T(8,128)S(1)}, u32[]{:S(2)}, u32[]{:S(2)}) %collective-permute-start.12) | collective-permute-done | bytes 131104 | tf_op jit(solution)/shard_map/ppermute | solution.py:25
  90.3 3.0 %shard_map.127 = (f32[64,2048]{1,0:T(8,128)S(1)}, f32[64,2048]{1,0:T(8,128)S(1)}, f32[64,512]{1,0:T(8,128)S(1)}, f32[64,512]{1,0:T(8,128)S(1)}, f32[64,512]{1,0:...) custom-call(s32[4]{0:T(128)S(1)} %pad_add_fusion.order, f32[64,512]{1,0:T(8,128)S(1)} %collective-permute-done.9.refs_0_, ...), custom_call_target="tpu_custom_call" | custom-call | flops 536870912 | bytes 2926592 | tf_op jit(solution)/shard_map/pallas_call | solution.py:322
  93.4 20.9 %all_to_all.25 = f32[64,16,128]{2,1,0:T(8,128)S(1)} all-to-all(f32[64,16,128]{2,1,0:T(8,128)S(1)} %broadcast_in_dim.13), channel_id=1, replica_groups={{0,1,2,3,4,5,6,7,8,9,10,11,12,13,14,15,32,33,34,35,36,37,38,39,40,41,42..., dimensions={0} | all-to-all | bytes 1048576 | tf_op jit(solution)/shard_map/all_to_all | solution.py:429
  115.6 2.4 %collective-permute-start.13 = (f32[456,128]{1,0:T(8,128)S(1)}, f32[456,128]{1,0:T(8,128)S(1)}, u32[]{:S(2)}, u32[]{:S(2)}) collective-permute-start(f32[456,128]{1,0:T(8,128)S(1)} %shard_map.128.refs_0_), channel_id=1, source_target_pairs={{0,16},{16,0},{32,48},{48,32},{64,80},{80,64},{96,112},{112,96},{1... | collective-permute-start | bytes 700424 | tf_op jit(solution)/shard_map/ppermute | solution.py:25
  122.8 3.0 %collective-permute-done.17.refs_4_ = f32[64,512]{1,0:T(8,128)S(1)} collective-permute-done((f32[64,512]{1,0:T(8,128)S(1)}, f32[64,512]{1,0:T(8,128)S(1)}, u32[]{:S(2)}, u32[]{:S(2)}) %collective-permute-start.17) | collective-permute-done | bytes 131104 | tf_op jit(solution)/shard_map/ppermute | solution.py:25
  125.8 3.0 %shard_map.130 = (f32[64,2048]{1,0:T(8,128)S(1)}, f32[64,2048]{1,0:T(8,128)S(1)}, f32[64,512]{1,0:T(8,128)S(1)}, f32[64,512]{1,0:T(8,128)S(1)}, f32[64,512]{1,0:...) custom-call(s32[4]{0:T(128)S(1)} %pad_add_fusion.order, ...), custom_call_target="tpu_custom_call" | custom-call | flops 536870912 | bytes 3375104 | tf_op jit(solution)/shard_map/pallas_call | solution.py:322
  128.8 2.2 %collective-permute-start.18 = (f32[64,512]{1,0:T(8,128)S(1)}, f32[64,512]{1,0:T(8,128)S(1)}, u32[]{:S(2)}, u32[]{:S(2)}) collective-permute-start(f32[64,512]{1,0:T(8,128)S(1)} %get-tuple-element.113), channel_id=1, source_target_pairs={{0,16},{16,0},{32,48},{48,32},{64,80},{80,64},{96,112},{112,96},{1... | collective-permute-start | bytes 393224 | tf_op jit(solution)/shard_map/ppermute | solution.py:25
  133.0 2.7 %collective-permute-done.19.refs_1_ = f32[64,512]{1,0:T(8,128)S(1)} collective-permute-done((f32[64,512]{1,0:T(8,128)S(1)}, f32[64,512]{1,0:T(8,128)S(1)}, u32[]{:S(2)}, u32[]{:S(2)}) %collective-permute-start.19) | collective-permute-done | bytes 131104 | tf_op jit(solution)/shard_map/ppermute | solution.py:25
  136.6 3.3 %collective-permute-done.21.refs_3_ = f32[64,512]{1,0:T(8,128)S(1)} collective-permute-done((f32[64,512]{1,0:T(8,128)S(1)}, f32[64,512]{1,0:T(8,128)S(1)}, u32[]{:S(2)}, u32[]{:S(2)}) %collective-permute-start.21) | collective-permute-done | bytes 131104 | tf_op jit(solution)/shard_map/ppermute | solution.py:25
  139.9 2.9 %shard_map.131 = (f32[64,2048]{1,0:T(8,128)S(1)}, f32[64,2048]{1,0:T(8,128)S(1)}, f32[64,512]{1,0:T(8,128)S(1)}, f32[64,512]{1,0:T(8,128)S(1)}, f32[64,512]{1,0:...) custom-call(s32[4]{0:T(128)S(1)} %pad_add_fusion.order, f32[64,512]{1,0:T(8,128)S(1)} %collective-permute-done.18.refs_0_, ...), custom_call_target="tpu_custom_call" | custom-call | flops 536870912 | bytes 3057664 | tf_op jit(solution)/shard_map/pallas_call | solution.py:322
  142.9 17.6 %all_to_all.26 = f32[64,16,128]{2,1,0:T(8,128)S(1)} all-to-all(f32[64,16,128]{2,1,0:T(8,128)S(1)} %broadcast_in_dim.14), channel_id=1, replica_groups={{0,1,2,3,4,5,6,7,8,9,10,11,12,13,14,15,32,33,34,35,36,37,38,39,40,41,42..., dimensions={0} | all-to-all | bytes 1048576 | tf_op jit(solution)/shard_map/all_to_all | solution.py:429
  161.8 2.4 %collective-permute-start.22 = (f32[456,128]{1,0:T(8,128)S(1)}, f32[456,128]{1,0:T(8,128)S(1)}, u32[]{:S(2)}, u32[]{:S(2)}) collective-permute-start(f32[456,128]{1,0:T(8,128)S(1)} %shard_map.132.refs_0_), channel_id=1, source_target_pairs={{0,16},{16,0},{32,48},{48,32},{64,80},{80,64},{96,112},{112,96},{1... | collective-permute-start | bytes 700424 | tf_op jit(solution)/shard_map/ppermute | solution.py:25
  166.3 1.7 shard_map.133
  169.0 3.0 %collective-permute-done.26.refs_4_ = f32[64,512]{1,0:T(8,128)S(1)} collective-permute-done((f32[64,512]{1,0:T(8,128)S(1)}, f32[64,512]{1,0:T(8,128)S(1)}, u32[]{:S(2)}, u32[]{:S(2)}) %collective-permute-start.26) | collective-permute-done | bytes 131104 | tf_op jit(solution)/shard_map/ppermute | solution.py:25
  172.0 3.3 %shard_map.134 = (f32[64,2048]{1,0:T(8,128)}, f32[64,2048]{1,0:T(8,128)S(1)}, f32[64,512]{1,0:T(8,128)S(1)}, f32[64,512]{1,0:T(8,128)S(1)}, f32[64,512]{1,0:T(8,...) custom-call(s32[4]{0:T(128)S(1)} %pad_add_fusion.order, f32[160,128]{1,0:T(8,128)S(1)} %get-tuple-element.122.refs_0_, ...), custom_call_target="tpu_custom_call" | custom-call | flops 536870912 | bytes 3645440 | tf_op jit(solution)/shard_map/pallas_call | solution.py:322
  175.3 2.2 %collective-permute-start.27 = (f32[64,512]{1,0:T(8,128)S(1)}, f32[64,512]{1,0:T(8,128)S(1)}, u32[]{:S(2)}, u32[]{:S(2)}) collective-permute-start(f32[64,512]{1,0:T(8,128)S(1)} %get-tuple-element.136), channel_id=1, source_target_pairs={{0,16},{16,0},{32,48},{48,32},{64,80},{80,64},{96,112},{112,96},{1... | collective-permute-start | bytes 393224 | tf_op jit(solution)/shard_map/ppermute | solution.py:25
  179.4 2.8 %collective-permute-done.28.refs_1_ = f32[64,512]{1,0:T(8,128)S(1)} collective-permute-done((f32[64,512]{1,0:T(8,128)S(1)}, f32[64,512]{1,0:T(8,128)S(1)}, u32[]{:S(2)}, u32[]{:S(2)}) %collective-permute-start.28) | collective-permute-done | bytes 131104 | tf_op jit(solution)/shard_map/ppermute | solution.py:25
  183.0 3.3 %collective-permute-done.30.refs_3_ = f32[64,512]{1,0:T(8,128)S(1)} collective-permute-done((f32[64,512]{1,0:T(8,128)S(1)}, f32[64,512]{1,0:T(8,128)S(1)}, u32[]{:S(2)}, u32[]{:S(2)}) %collective-permute-start.30) | collective-permute-done | bytes 131104 | tf_op jit(solution)/shard_map/ppermute | solution.py:25
  186.3 1.8 shard_map.135
  (110 shorter events, 38.8 us)
Async XLA Ops:
  7.2 62.2 %all-gather.2.cloned.1.call-start = ((), (), s32[]{:S(2)}) async-start(), calls=%async_computation.3 | async-start | bytes 3411968 | tf_op jit(solution)/shard_map/all_gather | solution.py:365
  12.8 18.3 %collective-permute-start = (f32[104,512]{1,0:T(8,128)S(1)}, f32[104,512]{1,0:T(8,128)S(1)}, u32[]{:S(2)}, u32[]{:S(2)}) collective-permute-start(f32[104,512]{1,0:T(8,128)S(1)} %get-tuple-element.78), channel_id=1, source_target_pairs={{0,16},{16,0},{32,48},{48,32},{64,80},{80,64},{96,112},{112,96},{1... | collective-permute-start | bytes 638984 | tf_op jit(solution)/shard_map/ppermute | solution.py:25
  14.3 16.8 %collective-permute-start.1 = (f32[104,512]{1,0:T(8,128)S(1)}, f32[104,512]{1,0:T(8,128)S(1)}, u32[]{:S(2)}, u32[]{:S(2)}) collective-permute-start(f32[104,512]{1,0:T(8,128)S(1)} %get-tuple-element.79), channel_id=1, source_target_pairs={{16,32},{32,16},{48,64},{64,48},{80,96},{96,80},{112,0},{0,112},{1... | collective-permute-start | bytes 638984 | tf_op jit(solution)/shard_map/ppermute | solution.py:25
  15.6 15.4 %collective-permute-start.2 = (f32[104,512]{1,0:T(8,128)S(1)}, f32[104,512]{1,0:T(8,128)S(1)}, u32[]{:S(2)}, u32[]{:S(2)}) collective-permute-start(f32[104,512]{1,0:T(8,128)S(1)} %get-tuple-element.80), channel_id=1, source_target_pairs={{0,1},{1,0},{2,3},{3,2},{4,5},{5,4},{6,7},{7,6},{8,9},{9,8},{10,11... | collective-permute-start | bytes 638984 | tf_op jit(solution)/shard_map/ppermute | solution.py:25
  17.3 13.8 %collective-permute-start.3 = (f32[104,512]{1,0:T(8,128)S(1)}, f32[104,512]{1,0:T(8,128)S(1)}, u32[]{:S(2)}, u32[]{:S(2)}) collective-permute-start(f32[104,512]{1,0:T(8,128)S(1)} %get-tuple-element.81), channel_id=1, source_target_pairs={{1,2},{2,1},{3,4},{4,3},{5,6},{6,5},{7,8},{8,7},{9,10},{10,9},{11,... | collective-permute-start | bytes 638984 | tf_op jit(solution)/shard_map/ppermute | solution.py:25
  62.4 6.3 %collective-permute-start.4 = (f32[456,128]{1,0:T(8,128)S(1)}, f32[456,128]{1,0:T(8,128)S(1)}, u32[]{:S(2)}, u32[]{:S(2)}) collective-permute-start(f32[456,128]{1,0:T(8,128)S(1)} %get-tuple-element.84.refs_0_), channel_id=1, source_target_pairs={{0,16},{16,0},{32,48},{48,32},{64,80},{80,64},{96,112},{112,96},{1... | collective-permute-start | bytes 700424 | tf_op jit(solution)/shard_map/ppermute | solution.py:25
  66.8 9.9 %collective-permute-start.5 = (f32[64,512]{1,0:T(8,128)}, f32[64,512]{1,0:T(8,128)}, u32[]{:S(2)}, u32[]{:S(2)}) collective-permute-start(f32[64,512]{1,0:T(8,128)} %get-tuple-element.87), channel_id=1, source_target_pairs={{0,16},{16,0},{32,48},{48,32},{64,80},{80,64},{96,112},{112,96},{1... | collective-permute-start | bytes 393224 | tf_op jit(solution)/shard_map/ppermute | solution.py:25
  66.8 9.9 %collective-permute-start.6 = (f32[64,512]{1,0:T(8,128)}, f32[64,512]{1,0:T(8,128)}, u32[]{:S(2)}, u32[]{:S(2)}) collective-permute-start(f32[64,512]{1,0:T(8,128)} %get-tuple-element.88), channel_id=1, source_target_pairs={{16,32},{32,16},{48,64},{64,48},{80,96},{96,80},{112,0},{0,112},{1... | collective-permute-start | bytes 393224 | tf_op jit(solution)/shard_map/ppermute | solution.py:25
  66.8 9.9 %collective-permute-start.7 = (f32[64,512]{1,0:T(8,128)}, f32[64,512]{1,0:T(8,128)}, u32[]{:S(2)}, u32[]{:S(2)}) collective-permute-start(f32[64,512]{1,0:T(8,128)} %get-tuple-element.89), channel_id=1, source_target_pairs={{0,1},{1,0},{2,3},{3,2},{4,5},{5,4},{6,7},{7,6},{8,9},{9,8},{10,11... | collective-permute-start | bytes 393224 | tf_op jit(solution)/shard_map/ppermute | solution.py:25
  67.3 9.5 %collective-permute-start.8 = (f32[64,512]{1,0:T(8,128)}, f32[64,512]{1,0:T(8,128)}, u32[]{:S(2)}, u32[]{:S(2)}) collective-permute-start(f32[64,512]{1,0:T(8,128)} %get-tuple-element.90), channel_id=1, source_target_pairs={{1,2},{2,1},{3,4},{4,3},{5,6},{6,5},{7,8},{8,7},{9,10},{10,9},{11,... | collective-permute-start | bytes 393224 | tf_op jit(solution)/shard_map/ppermute | solution.py:25
  81.0 5.8 %collective-permute-start.9 = (f32[64,512]{1,0:T(8,128)S(1)}, f32[64,512]{1,0:T(8,128)S(1)}, u32[]{:S(2)}, u32[]{:S(2)}) collective-permute-start(f32[64,512]{1,0:T(8,128)S(1)} %get-tuple-element.93), channel_id=1, source_target_pairs={{0,16},{16,0},{32,48},{48,32},{64,80},{80,64},{96,112},{112,96},{1... | collective-permute-start | bytes 393224 | tf_op jit(solution)/shard_map/ppermute | solution.py:25
  82.1 4.7 %collective-permute-start.10 = (f32[64,512]{1,0:T(8,128)S(1)}, f32[64,512]{1,0:T(8,128)S(1)}, u32[]{:S(2)}, u32[]{:S(2)}) collective-permute-start(f32[64,512]{1,0:T(8,128)S(1)} %get-tuple-element.94), channel_id=1, source_target_pairs={{16,32},{32,16},{48,64},{64,48},{80,96},{96,80},{112,0},{0,112},{1... | collective-permute-start | bytes 393224 | tf_op jit(solution)/shard_map/ppermute | solution.py:25
  83.2 4.1 %collective-permute-start.11 = (f32[64,512]{1,0:T(8,128)S(1)}, f32[64,512]{1,0:T(8,128)S(1)}, u32[]{:S(2)}, u32[]{:S(2)}) collective-permute-start(f32[64,512]{1,0:T(8,128)S(1)} %get-tuple-element.95), channel_id=1, source_target_pairs={{0,1},{1,0},{2,3},{3,2},{4,5},{5,4},{6,7},{7,6},{8,9},{9,8},{10,11... | collective-permute-start | bytes 393224 | tf_op jit(solution)/shard_map/ppermute | solution.py:25
  83.2 7.1 %collective-permute-start.12 = (f32[64,512]{1,0:T(8,128)S(1)}, f32[64,512]{1,0:T(8,128)S(1)}, u32[]{:S(2)}, u32[]{:S(2)}) collective-permute-start(f32[64,512]{1,0:T(8,128)S(1)} %get-tuple-element.96), channel_id=1, source_target_pairs={{1,2},{2,1},{3,4},{4,3},{5,6},{6,5},{7,8},{8,7},{9,10},{10,9},{11,... | collective-permute-start | bytes 393224 | tf_op jit(solution)/shard_map/ppermute | solution.py:25
  115.6 4.5 %collective-permute-start.13 = (f32[456,128]{1,0:T(8,128)S(1)}, f32[456,128]{1,0:T(8,128)S(1)}, u32[]{:S(2)}, u32[]{:S(2)}) collective-permute-start(f32[456,128]{1,0:T(8,128)S(1)} %shard_map.128.refs_0_), channel_id=1, source_target_pairs={{0,16},{16,0},{32,48},{48,32},{64,80},{80,64},{96,112},{112,96},{1... | collective-permute-start | bytes 700424 | tf_op jit(solution)/shard_map/ppermute | solution.py:25
  118.0 3.7 %collective-permute-start.14 = (f32[64,512]{1,0:T(8,128)S(1)}, f32[64,512]{1,0:T(8,128)S(1)}, u32[]{:S(2)}, u32[]{:S(2)}) collective-permute-start(f32[64,512]{1,0:T(8,128)S(1)} %get-tuple-element.104), channel_id=1, source_target_pairs={{0,16},{16,0},{32,48},{48,32},{64,80},{80,64},{96,112},{112,96},{1... | collective-permute-start | bytes 393224 | tf_op jit(solution)/shard_map/ppermute | solution.py:25
  118.1 4.7 %collective-permute-start.15 = (f32[64,512]{1,0:T(8,128)S(1)}, f32[64,512]{1,0:T(8,128)S(1)}, u32[]{:S(2)}, u32[]{:S(2)}) collective-permute-start(f32[64,512]{1,0:T(8,128)S(1)} %get-tuple-element.105), channel_id=1, source_target_pairs={{16,32},{32,16},{48,64},{64,48},{80,96},{96,80},{112,0},{0,112},{1... | collective-permute-start | bytes 393224 | tf_op jit(solution)/shard_map/ppermute | solution.py:25
  118.3 4.5 %collective-permute-start.16 = (f32[64,512]{1,0:T(8,128)S(1)}, f32[64,512]{1,0:T(8,128)S(1)}, u32[]{:S(2)}, u32[]{:S(2)}) collective-permute-start(f32[64,512]{1,0:T(8,128)S(1)} %get-tuple-element.106), channel_id=1, source_target_pairs={{0,1},{1,0},{2,3},{3,2},{4,5},{5,4},{6,7},{7,6},{8,9},{9,8},{10,11... | collective-permute-start | bytes 393224 | tf_op jit(solution)/shard_map/ppermute | solution.py:25
  118.7 7.1 %collective-permute-start.17 = (f32[64,512]{1,0:T(8,128)S(1)}, f32[64,512]{1,0:T(8,128)S(1)}, u32[]{:S(2)}, u32[]{:S(2)}) collective-permute-start(f32[64,512]{1,0:T(8,128)S(1)} %get-tuple-element.107), channel_id=1, source_target_pairs={{1,2},{2,1},{3,4},{4,3},{5,6},{6,5},{7,8},{8,7},{9,10},{10,9},{11,... | collective-permute-start | bytes 393224 | tf_op jit(solution)/shard_map/ppermute | solution.py:25
  128.8 4.2 %collective-permute-start.18 = (f32[64,512]{1,0:T(8,128)S(1)}, f32[64,512]{1,0:T(8,128)S(1)}, u32[]{:S(2)}, u32[]{:S(2)}) collective-permute-start(f32[64,512]{1,0:T(8,128)S(1)} %get-tuple-element.113), channel_id=1, source_target_pairs={{0,16},{16,0},{32,48},{48,32},{64,80},{80,64},{96,112},{112,96},{1... | collective-permute-start | bytes 393224 | tf_op jit(solution)/shard_map/ppermute | solution.py:25
  131.0 4.7 %collective-permute-start.19 = (f32[64,512]{1,0:T(8,128)S(1)}, f32[64,512]{1,0:T(8,128)S(1)}, u32[]{:S(2)}, u32[]{:S(2)}) collective-permute-start(f32[64,512]{1,0:T(8,128)S(1)} %get-tuple-element.114), channel_id=1, source_target_pairs={{16,32},{32,16},{48,64},{64,48},{80,96},{96,80},{112,0},{0,112},{1... | collective-permute-start | bytes 393224 | tf_op jit(solution)/shard_map/ppermute | solution.py:25
  131.9 4.7 %collective-permute-start.20 = (f32[64,512]{1,0:T(8,128)S(1)}, f32[64,512]{1,0:T(8,128)S(1)}, u32[]{:S(2)}, u32[]{:S(2)}) collective-permute-start(f32[64,512]{1,0:T(8,128)S(1)} %get-tuple-element.115), channel_id=1, source_target_pairs={{0,1},{1,0},{2,3},{3,2},{4,5},{5,4},{6,7},{7,6},{8,9},{9,8},{10,11... | collective-permute-start | bytes 393224 | tf_op jit(solution)/shard_map/ppermute | solution.py:25
  131.9 8.0 %collective-permute-start.21 = (f32[64,512]{1,0:T(8,128)S(1)}, f32[64,512]{1,0:T(8,128)S(1)}, u32[]{:S(2)}, u32[]{:S(2)}) collective-permute-start(f32[64,512]{1,0:T(8,128)S(1)} %get-tuple-element.116), channel_id=1, source_target_pairs={{1,2},{2,1},{3,4},{4,3},{5,6},{6,5},{7,8},{8,7},{9,10},{10,9},{11,... | collective-permute-start | bytes 393224 | tf_op jit(solution)/shard_map/ppermute | solution.py:25
  161.8 4.5 %collective-permute-start.22 = (f32[456,128]{1,0:T(8,128)S(1)}, f32[456,128]{1,0:T(8,128)S(1)}, u32[]{:S(2)}, u32[]{:S(2)}) collective-permute-start(f32[456,128]{1,0:T(8,128)S(1)} %shard_map.132.refs_0_), channel_id=1, source_target_pairs={{0,16},{16,0},{32,48},{48,32},{64,80},{80,64},{96,112},{112,96},{1... | collective-permute-start | bytes 700424 | tf_op jit(solution)/shard_map/ppermute | solution.py:25
  164.2 3.8 %collective-permute-start.23 = (f32[64,512]{1,0:T(8,128)S(1)}, f32[64,512]{1,0:T(8,128)S(1)}, u32[]{:S(2)}, u32[]{:S(2)}) collective-permute-start(f32[64,512]{1,0:T(8,128)S(1)} %get-tuple-element.123), channel_id=1, source_target_pairs={{0,16},{16,0},{32,48},{48,32},{64,80},{80,64},{96,112},{112,96},{1... | collective-permute-start | bytes 393224 | tf_op jit(solution)/shard_map/ppermute | solution.py:25
  164.3 4.7 %collective-permute-start.24 = (f32[64,512]{1,0:T(8,128)S(1)}, f32[64,512]{1,0:T(8,128)S(1)}, u32[]{:S(2)}, u32[]{:S(2)}) collective-permute-start(f32[64,512]{1,0:T(8,128)S(1)} %get-tuple-element.124), channel_id=1, source_target_pairs={{16,32},{32,16},{48,64},{64,48},{80,96},{96,80},{112,0},{0,112},{1... | collective-permute-start | bytes 393224 | tf_op jit(solution)/shard_map/ppermute | solution.py:25
  164.5 4.5 %collective-permute-start.25 = (f32[64,512]{1,0:T(8,128)S(1)}, f32[64,512]{1,0:T(8,128)S(1)}, u32[]{:S(2)}, u32[]{:S(2)}) collective-permute-start(f32[64,512]{1,0:T(8,128)S(1)} %get-tuple-element.125), channel_id=1, source_target_pairs={{0,1},{1,0},{2,3},{3,2},{4,5},{5,4},{6,7},{7,6},{8,9},{9,8},{10,11... | collective-permute-start | bytes 393224 | tf_op jit(solution)/shard_map/ppermute | solution.py:25
  164.9 7.1 %collective-permute-start.26 = (f32[64,512]{1,0:T(8,128)S(1)}, f32[64,512]{1,0:T(8,128)S(1)}, u32[]{:S(2)}, u32[]{:S(2)}) collective-permute-start(f32[64,512]{1,0:T(8,128)S(1)} %get-tuple-element.126), channel_id=1, source_target_pairs={{1,2},{2,1},{3,4},{4,3},{5,6},{6,5},{7,8},{8,7},{9,10},{10,9},{11,... | collective-permute-start | bytes 393224 | tf_op jit(solution)/shard_map/ppermute | solution.py:25
  175.3 4.1 %collective-permute-start.27 = (f32[64,512]{1,0:T(8,128)S(1)}, f32[64,512]{1,0:T(8,128)S(1)}, u32[]{:S(2)}, u32[]{:S(2)}) collective-permute-start(f32[64,512]{1,0:T(8,128)S(1)} %get-tuple-element.136), channel_id=1, source_target_pairs={{0,16},{16,0},{32,48},{48,32},{64,80},{80,64},{96,112},{112,96},{1... | collective-permute-start | bytes 393224 | tf_op jit(solution)/shard_map/ppermute | solution.py:25
  177.5 4.7 %collective-permute-start.28 = (f32[64,512]{1,0:T(8,128)S(1)}, f32[64,512]{1,0:T(8,128)S(1)}, u32[]{:S(2)}, u32[]{:S(2)}) collective-permute-start(f32[64,512]{1,0:T(8,128)S(1)} %get-tuple-element.137), channel_id=1, source_target_pairs={{16,32},{32,16},{48,64},{64,48},{80,96},{96,80},{112,0},{0,112},{1... | collective-permute-start | bytes 393224 | tf_op jit(solution)/shard_map/ppermute | solution.py:25
  178.3 4.7 %collective-permute-start.29 = (f32[64,512]{1,0:T(8,128)S(1)}, f32[64,512]{1,0:T(8,128)S(1)}, u32[]{:S(2)}, u32[]{:S(2)}) collective-permute-start(f32[64,512]{1,0:T(8,128)S(1)} %get-tuple-element.138), channel_id=1, source_target_pairs={{0,1},{1,0},{2,3},{3,2},{4,5},{5,4},{6,7},{7,6},{8,9},{9,8},{10,11... | collective-permute-start | bytes 393224 | tf_op jit(solution)/shard_map/ppermute | solution.py:25
  178.3 8.0 %collective-permute-start.30 = (f32[64,512]{1,0:T(8,128)S(1)}, f32[64,512]{1,0:T(8,128)S(1)}, u32[]{:S(2)}, u32[]{:S(2)}) collective-permute-start(f32[64,512]{1,0:T(8,128)S(1)} %get-tuple-element.139), channel_id=1, source_target_pairs={{1,2},{2,1},{3,4},{4,3},{5,6},{6,5},{7,8},{8,7},{9,10},{10,9},{11,... | collective-permute-start | bytes 393224 | tf_op jit(solution)/shard_map/ppermute | solution.py:25
  (23 other events, 130.3 us)
Sparse Core Ops, SparseCore 0:
  10.2 56.2 all-gather.1
